TPU v7x, 256 devices: a whole 4x4x8 slice. The times are simulated.
256 devices in a mesh: energy: 64 (over z, x, core), slab: 4 (over y).
Axes of the slice: x: 4, y: 4, z: 8, core: 2. Of those that a mesh axis runs over, the one named last changes fastest.
Arguments:
- green: bfloat16 [2048, 36864], P('energy', 'slab'), may hold values from -1.75 to 1.75
- sigma_in: bfloat16 [2048, 36864], P('energy', 'slab'), may hold values from -6 to 6
- neighbours: int32 [256, 8], P('slab'), may hold values from 0 to 95
- coupling: float32 [256, 8], P('slab'), may hold values from 0.1 to 1
- send_down: int32 [4, 16], P('slab'), may hold values from 0 to 63, as said below
- send_up: int32 [4, 16], P('slab'), may hold values from 0 to 63, as said below
- offsets: int32 [16], replicated, may hold values from 1 to 32, as said below
- w_emit: float32 [16], replicated, may hold values from 0.02 to 0.2
- w_absorb: float32 [16], replicated, may hold values from 0.02 to 0.2
Outputs:
- sigma_ph: bfloat16 [2048, 36864], P('energy', 'slab')
- g_less: bfloat16 [2048, 36864], P('energy', 'slab')
Inputs may be any that keep to these rules, and one draw needn't show every extreme that they name: Each row of send_down holds 16 distinct atom numbers of one slab. Each row of send_up holds 16 distinct atom numbers of one slab. The 16 offsets are distinct, and 32 is one of them.
All inputs are finite; a program needn't handle non-finite values.
Results may differ from a plain program's by a relative error of at most 0.0063.
Values may be sent and summed in bfloat16 or wider, within the bound.
No kernel may reach another device: no remote copies, remote signals or barrier semaphores. Data moves between devices by JAX's collectives and lax.ppermute only.
A program may use at most 128 MiB of HBM per device.

v0:
```python
import jax
import jax.numpy as jnp
from jax import lax
from jax.experimental import pallas as pl
from jax.experimental.pallas import tpu as pltpu
from jax.sharding import PartitionSpec as P

ORB = 12
PAIRS = 144
NBRS = 8
LANES = 128
GROUPS = 4
ROWS = 32
NEAR = 16
SPAN = NEAR * PAIRS
TILES = SPAN // LANES
QUADS = PAIRS // GROUPS
WIDTH = PAIRS * ROWS
F32 = jnp.float32
BF16 = jnp.bfloat16


def lane_iota(shape):
    return lax.broadcasted_iota(jnp.int32, shape, len(shape) - 1)


def row_iota(shape):
    return lax.broadcasted_iota(jnp.int32, shape, len(shape) - 2)


def identity():
    return (lane_iota((LANES, LANES)) == row_iota((LANES, LANES))).astype(BF16)


def flip(eye, tile):
    return lax.dot_general(eye, tile, (((1,), (1,)), ((), ())), preferred_element_type=F32)


def to_batch_lanes(source, flat, target):
    eye = identity()

    for t in range(TILES):
        columns = [source[:, h * SPAN + t * LANES : h * SPAN + (t + 1) * LANES] for h in range(GROUPS)]
        flat[t * LANES : (t + 1) * LANES, :] = flip(eye, jnp.concatenate(columns, axis=0))

    for p in range(PAIRS):
        for g in range(2):
            target[p, 8 * g : 8 * g + 8, :] = flat[pl.ds(8 * g * PAIRS + p, 8, stride=PAIRS), :]


def to_energy_rows(flat, target):
    eye = identity()

    for t in range(TILES):
        turned = flip(eye, flat[t * LANES : (t + 1) * LANES, :].astype(BF16)).astype(BF16)
        for h in range(GROUPS):
            column = h * SPAN + t * LANES
            target[:, column : column + LANES] = turned[h * ROWS : (h + 1) * ROWS]


def sandwich(left, middle, store):
    depth = 3

    def body(step, carry):
        g = step % 2
        first = (step // 2) * depth
        half = pl.ds(pl.multiple_of(g * 8, 8), 8)
        product = [[None] * ORB for _ in range(depth)]
        for j in range(ORB):
            lhs = [left[(first + r) * ORB + j, half, :] for r in range(depth)]
            for k in range(ORB):
                rhs = middle[j * ORB + k, half, :]
                for r in range(depth):
                    term = lhs[r] * rhs
                    product[r][k] = term if j == 0 else product[r][k] + term
        for l in range(ORB):
            total = [None] * depth
            for k in range(ORB):
                rhs = left[l * ORB + k, half, :]
                for r in range(depth):
                    term = product[r][k] * rhs
                    total[r] = term if k == 0 else total[r] + term
            for r in range(depth):
                store((first + r) * ORB + l, g, half, total[r])
        return carry

    lax.fori_loop(0, 2 * ORB // depth, body, 0)


def swap_chunks(values):
    chunk = lane_iota(values[0].shape) // ROWS
    low = chunk % 2 == 0
    out = list(values)
    for a, b in ((0, 1), (2, 3)):
        x, y = out[a], out[b]
        out[a] = jnp.where(low, x, pltpu.roll(y, ROWS, 1))
        out[b] = jnp.where(low, pltpu.roll(x, LANES - ROWS, 1), y)
    low = chunk < 2
    for a, b in ((0, 2), (1, 3)):
        x, y = out[a], out[b]
        out[a] = jnp.where(low, x, pltpu.roll(y, 2 * ROWS, 1))
        out[b] = jnp.where(low, pltpu.roll(x, LANES - 2 * ROWS, 1), y)
    return out


def lesser_kernel(green, sigma_in, first_list, second_list, green_t, sigma_t, own, first, second, flat, result):
    to_batch_lanes(green, flat, green_t)
    to_batch_lanes(sigma_in, flat, sigma_t)

    def store(p, g, half, value):
        result[p, half, :] = value

    sandwich(green_t, sigma_t, store)

    def regroup(q, carry):
        parts = swap_chunks([result[GROUPS * q + j] for j in range(GROUPS)])
        columns = pl.ds(pl.multiple_of(q * LANES, LANES), LANES)
        for h in range(GROUPS):
            own[h * NEAR : (h + 1) * NEAR, columns] = parts[h].astype(BF16)
        return carry

    lax.fori_loop(0, QUADS, regroup, 0, unroll=4)
    for listed, target in ((first_list, first), (second_list, second)):
        pick = (row_iota((64, 16)) == listed[...]).astype(BF16)
        for t in range(WIDTH // 512):
            columns = slice(t * 512, (t + 1) * 512)
            target[:, columns] = lax.dot_general(
                pick, own[:, columns], (((0,), (0,)), ((), ())), preferred_element_type=F32
            ).astype(BF16)


def mix_kernel(neighbours, coupling, own, low, high, mixed):
    names = lane_iota((64, 96))
    weights = jnp.zeros((64, 96), F32)
    for k in range(NBRS):
        weights = weights + jnp.where(names == neighbours[:, k : k + 1], coupling[:, k : k + 1], 0.0)
    coarse = weights.astype(BF16)
    fine = (weights - coarse.astype(F32)).astype(BF16)
    both = jnp.concatenate([coarse, fine], axis=1)
    for t in range(WIDTH // 512):
        columns = slice(t * 512, (t + 1) * 512)
        listed = [own[:, columns], low[:, columns], high[:, columns]]
        extended = jnp.concatenate(listed + listed, axis=0)
        mixed[:, columns] = jnp.dot(both, extended, preferred_element_type=F32).astype(BF16)


def band(offsets, w_emit, w_absorb):
    shape = (ROWS, LANES)
    distance = lane_iota(shape) % ROWS - row_iota(shape)
    before = jnp.zeros(shape, F32)
    here = jnp.zeros(shape, F32)
    after = jnp.zeros(shape, F32)
    for w in range(16):
        off, emit, absorb = offsets[w], w_emit[w], w_absorb[w]
        before = before + jnp.where(distance + ROWS == off, emit, 0.0)
        here = here + jnp.where(distance == off, emit, 0.0) + jnp.where(-distance == off, absorb, 0.0)
        after = after + jnp.where(ROWS - distance == off, absorb, 0.0)
    group = lane_iota(shape) // ROWS
    parts = []
    for block in (before, here, after):
        parts += [jnp.where(group == h, block, 0.0) for h in range(GROUPS)]
    return jnp.concatenate(parts, axis=0).astype(BF16)


def final_kernel(offsets, w_emit, w_absorb, green_t, sigma_t, before, here, after, sigma_ph, g_less, flat, middle, matrix):
    matrix[...] = band(offsets, w_emit, w_absorb)

    def convolve(q, carry):
        columns = pl.ds(pl.multiple_of(q * LANES, LANES), LANES)
        lhs = jnp.concatenate([before[:, columns], here[:, columns], after[:, columns]], axis=1)
        total = jnp.dot(lhs, matrix[...], preferred_element_type=F32).astype(BF16).astype(F32)
        parts = swap_chunks([total[h * NEAR : (h + 1) * NEAR] for h in range(GROUPS)])
        for j in range(GROUPS):
            p = GROUPS * q + j
            middle[p] = sigma_t[p] + parts[j]
            for g in range(2):
                flat[pl.ds(8 * g * PAIRS + p, 8, stride=PAIRS), :] = parts[j][8 * g : 8 * g + 8]
        return carry

    lax.fori_loop(0, QUADS, convolve, 0, unroll=4)
    to_energy_rows(flat, sigma_ph)

    def store(p, g, half, value):
        flat[pl.ds(g * 8 * PAIRS + p, 8, stride=PAIRS), :] = value

    sandwich(green_t, middle, store)
    to_energy_rows(flat, g_less)


def vmem(count):
    return [pl.BlockSpec(memory_space=pltpu.VMEM)] * count


def smem(count):
    return [pl.BlockSpec(memory_space=pltpu.SMEM)] * count


PARAMS = pltpu.CompilerParams(vmem_limit_bytes=48 * 1024 * 1024)


def swap(block, axis, parity):
    pairs = []
    for i in range(parity, lax.axis_size(axis) - 1, 2):
        pairs += [(i, i + 1), (i + 1, i)]
    return lax.ppermute(block, axis, pairs)


def on_device(green, sigma_in, neighbours, coupling, send_down, send_up, offsets, w_emit, w_absorb):
    odd_slab = lax.axis_index("slab") % 2 == 1
    odd_energy = lax.axis_index("energy") % 2 == 1
    first_list = jnp.where(odd_slab, send_down, send_up)
    second_list = jnp.where(odd_slab, send_up, send_down)
    whole = jax.ShapeDtypeStruct((PAIRS, NEAR, LANES), F32)
    edge = jax.ShapeDtypeStruct((16, WIDTH), BF16)
    block = jax.ShapeDtypeStruct((64, WIDTH), BF16)
    green_t, sigma_t, own, first, second = pl.pallas_call(
        lesser_kernel,
        out_shape=(whole, whole, block, edge, edge),
        in_specs=vmem(4),
        out_specs=tuple(vmem(5)),
        scratch_shapes=[pltpu.VMEM((SPAN, LANES), F32), pltpu.VMEM((PAIRS, NEAR, LANES), F32)],
        compiler_params=PARAMS,
    )(green, sigma_in, first_list, second_list)
    first = swap(first, "slab", 0)
    second = swap(second, "slab", 1)
    low = jnp.where(odd_slab, first, second)
    high = jnp.where(odd_slab, second, first)
    mixed = pl.pallas_call(
        mix_kernel,
        out_shape=block,
        in_specs=vmem(5),
        out_specs=vmem(1)[0],
        compiler_params=PARAMS,
    )(neighbours, coupling, own, low, high)
    apart = swap(mixed, "energy", 1)
    beside = swap(mixed, "energy", 0)
    before = jnp.where(odd_energy, beside, apart)
    after = jnp.where(odd_energy, apart, beside)
    flat = jax.ShapeDtypeStruct(green.shape, BF16)
    return pl.pallas_call(
        final_kernel,
        out_shape=(flat, flat),
        in_specs=smem(3) + vmem(5),
        out_specs=tuple(vmem(2)),
        scratch_shapes=[
            pltpu.VMEM((SPAN, LANES), F32),
            pltpu.VMEM((PAIRS, NEAR, LANES), F32),
            pltpu.VMEM((3 * LANES, LANES), BF16),
        ],
        compiler_params=PARAMS,
    )(offsets, w_emit, w_absorb, green_t, sigma_t, before, mixed, after)


def solution(mesh):
    split = P("energy", "slab")
    by_slab = P("slab", None)
    return jax.shard_map(
        on_device,
        mesh=mesh,
        in_specs=(split, split, by_slab, by_slab, by_slab, by_slab, P(), P(), P()),
        out_specs=(split, split),
        check_vma=False,
    )
```

profile of v0, /device:TPU:144, one launch (start us, length us, event | category | flops | bytes accessed | tf_op | source)
XLA Modules:
  0.0 43.1 jit_solution(11919771092345107992)
XLA Ops:
  0.6 0.0 copy-start.7
  0.6 0.0 copy-start.8
  0.7 0.7 %broadcast_select_fusion.4 = (s32[1,16]{1,0:T(1,128)S(1)}, s32[1,16]{1,0:T(1,128)S(1)}) fusion(s32[1,16]{1,0:T(1,128)} %param.14, s32[1,16]{1,0:T(1,128)} %param.13, pred[]{:T(512)S(6)} %eq.9), kind=kLoop, calls=%fused_computation.4 | loop fusion | flops 32 | bytes 257 | tf_op jit(solution)/shard_map/jit(_where)/select_n | solution.py:212
  1.3 0.0 copy-start
  1.3 1.1 %copy-done = bf16[32,9216]{1,0:T(8,128)(2,1)S(1)} copy-done((bf16[32,9216]{1,0:T(8,128)(2,1)S(1)}, bf16[32,9216]{1,0:T(8,128)(2,1)}, u32[]{:S(2)}) %copy-start) | copy-done | bytes 589848
  2.4 0.0 copy-start.1
  2.4 1.1 %copy-done.1 = bf16[32,9216]{1,0:T(8,128)(2,1)S(1)} copy-done((bf16[32,9216]{1,0:T(8,128)(2,1)S(1)}, bf16[32,9216]{1,0:T(8,128)(2,1)}, u32[]{:S(2)}) %copy-start.1) | copy-done | bytes 589848
  3.5 5.2 %shard_map.104 = (f32[144,16,128]{2,1,0:T(8,128)S(1)}, f32[144,16,128]{2,1,0:T(8,128)S(1)}, bf16[64,4608]{1,0:T(8,128)(2,1)S(1)}, bf16[16,4608]{1,0:T(8,128)(2,1)S(1)}, bf16[16,4608]{1,0:T(8,128)(2,1)S(1)}) custom-call(bf16[32,9216]{1,0:T(8,128)(2,1)S(1)} %copy-done, bf16[32,9216]{1,0:T(8,128)(2,1)S(1)} %copy-done.1, ...), custom_call_target="tpu_custom_call" | custom-call | tf_op jit(solution)/shard_map/pallas_call | solution.py:216
  8.7 1.4 %collective-permute-start = (bf16[16,4608]{1,0:T(8,128)(2,1)S(1)}, bf16[16,4608]{1,0:T(8,128)(2,1)S(1)}, u32[]{:S(2)}, u32[]{:S(2)}) collective-permute-start(bf16[16,4608]{1,0:T(8,128)(2,1)S(1)} %get-tuple-element.10), channel_id=1, source_target_pairs={{0,1},{1,0},{2,3},{3,2},{4,5},{5,4},{6,7},{7,6},{8,9},{9,8},{10,11... | collective-permute-start | bytes 442376 | tf_op jit(solution)/shard_map/ppermute | solution.py:205
  10.1 1.9 %collective-permute-start.1 = (bf16[16,4608]{1,0:T(8,128)(2,1)S(1)}, bf16[16,4608]{1,0:T(8,128)(2,1)S(1)}, u32[]{:S(2)}, u32[]{:S(2)}) collective-permute-start(bf16[16,4608]{1,0:T(8,128)(2,1)S(1)} %get-tuple-element.11), channel_id=1, source_target_pairs={{1,2},{2,1},{5,6},{6,5},{9,10},{10,9},{13,14},{14,13},{17,18},{18,... | collective-permute-start | bytes 442376 | tf_op jit(solution)/shard_map/ppermute | solution.py:205
  12.0 0.0 copy-done.7
  12.0 0.7 %copy.11.neighbours = s32[64,8]{1,0:T(8,128)} copy(s32[64,8]{0,1:T(8,128)S(1)} %copy-done.7) | data formatting | bytes 4096 | tf_op args[2]
  12.7 0.0 copy-done.8
  12.7 0.7 %copy.12.coupling = f32[64,8]{1,0:T(8,128)} copy(f32[64,8]{0,1:T(8,128)S(1)} %copy-done.8) | data formatting | bytes 4096 | tf_op args[3]
  13.4 1.0 %collective-permute-done = bf16[16,4608]{1,0:T(8,128)(2,1)S(1)} collective-permute-done((bf16[16,4608]{1,0:T(8,128)(2,1)S(1)}, bf16[16,4608]{1,0:T(8,128)(2,1)S(1)}, u32[]{:S(2)}, u32[]{:S(2)}) %collective-permute-start) | collective-permute-done | bytes 147488 | tf_op jit(solution)/shard_map/ppermute | solution.py:205
  14.4 2.9 %collective-permute-done.1 = bf16[16,4608]{1,0:T(8,128)(2,1)S(1)} collective-permute-done((bf16[16,4608]{1,0:T(8,128)(2,1)S(1)}, bf16[16,4608]{1,0:T(8,128)(2,1)S(1)}, u32[]{:S(2)}, u32[]{:S(2)}) %collective-permute-start.1) | collective-permute-done | bytes 147488 | tf_op jit(solution)/shard_map/ppermute | solution.py:205
  17.3 0.0 copy-start.2
  17.3 0.7 %copy-done.2 = s32[64,8]{1,0:T(8,128)S(1)} copy-done((s32[64,8]{1,0:T(8,128)S(1)}, s32[64,8]{1,0:T(8,128)}, u32[]{:S(2)}) %copy-start.2) | copy-done | bytes 2072
  18.0 0.0 copy-start.3
  18.0 0.8 %copy-done.3 = f32[64,8]{1,0:T(8,128)S(1)} copy-done((f32[64,8]{1,0:T(8,128)S(1)}, f32[64,8]{1,0:T(8,128)}, u32[]{:S(2)}) %copy-start.3) | copy-done | bytes 2072
  18.8 0.7 %shard_map.105.here = bf16[64,4608]{1,0:T(8,128)(2,1)S(1)} custom-call(s32[64,8]{1,0:T(8,128)S(1)} %copy-done.2, f32[64,8]{1,0:T(8,128)S(1)} %copy-done.3, bf16[64,4608]{1,0:T(8,128)(2,1)S(1)} %get-tuple-element.9.own, bf16[16,4608]{1,0:T(8,128)(2,1)S(1)} %get-tuple-element.15.low, bf16[16,4608]{1,0:T(8,128)(2,1)S(1)} %get-tuple-element.14.high), custom_call_target="tpu_custom_call" | custom-call | tf_op jit(solution)/shard_map/pallas_call | solution.py:228
  19.5 2.5 %collective-permute-start.3 = (bf16[64,4608]{1,0:T(8,128)(2,1)S(1)}, bf16[64,4608]{1,0:T(8,128)(2,1)S(1)}, u32[]{:S(2)}, u32[]{:S(2)}) collective-permute-start(bf16[64,4608]{1,0:T(8,128)(2,1)S(1)} %shard_map.105.here), channel_id=1, source_target_pairs={{4,8},{8,4},{12,16},{16,12},{20,24},{24,20},{28,32},{32,28},{36,40... | collective-permute-start | bytes 1769480 | tf_op jit(solution)/shard_map/ppermute | solution.py:205
  22.0 1.1 %collective-permute-start.2 = (bf16[64,4608]{1,0:T(8,128)(2,1)S(1)}, bf16[64,4608]{1,0:T(8,128)(2,1)}, u32[]{:S(2)}, u32[]{:S(2)}) collective-permute-start(bf16[64,4608]{1,0:T(8,128)(2,1)S(1)} %shard_map.105.here), channel_id=1, source_target_pairs={{0,4},{4,0},{8,12},{12,8},{16,20},{20,16},{24,28},{28,24},{32,36},... | collective-permute-start | bytes 1769480 | tf_op jit(solution)/shard_map/ppermute | solution.py:205
  23.1 0.0 copy-start.4
  23.1 0.0 copy-start.5
  23.1 0.0 copy-start.6
  23.1 10.9 %collective-permute-done.3 = bf16[64,4608]{1,0:T(8,128)(2,1)S(1)} collective-permute-done((bf16[64,4608]{1,0:T(8,128)(2,1)S(1)}, bf16[64,4608]{1,0:T(8,128)(2,1)S(1)}, u32[]{:S(2)}, u32[]{:S(2)}) %collective-permute-start.3) | collective-permute-done | bytes 589856 | tf_op jit(solution)/shard_map/ppermute | solution.py:205
  34.0 0.0 collective-permute-done.2
  34.0 1.1 %broadcast_select_fusion = (bf16[64,4608]{1,0:T(8,128)(2,1)S(1)}, bf16[64,4608]{1,0:T(8,128)(2,1)S(1)}) fusion(bf16[64,4608]{1,0:T(8,128)(2,1)S(1)} %collective-permute-done.3, bf16[64,4608]{1,0:T(8,128)(2,1)} %collective-permute-done.2, pred[]{:T(512)S(6)} %eq.10), kind=kLoop, calls=%fused_computation | loop fusion | flops 589824 | bytes 2359297 | tf_op jit(solution)/shard_map/jit(_where)/select_n | solution.py:238
  35.2 0.0 copy-done.4
  35.2 0.0 copy-done.5
  35.2 0.0 copy-done.6
  35.2 7.9 %shard_map.106 = (bf16[32,9216]{1,0:T(8,128)(2,1)}, bf16[32,9216]{1,0:T(8,128)(2,1)}) custom-call(s32[16]{0:T(128)S(1)} %copy-done.4, f32[16]{0:T(128)S(1)} %copy-done.5, f32[16]{0:T(128)S(1)} %copy-done.6, f32[144,16,128]{2,1,0:T(8,128)S(1)} %get-tuple-element.7.green_t, f32[144,16,128]{2,1,0:T(8,128)S(1)} %get-tuple-element.8.sigma_t, ...), custom_call_target="tpu_custom_call" | custom-call | tf_op jit(solution)/shard_map/pallas_call | solution.py:240
  (1 shorter events, 0.0 us)
Async XLA Ops:
  0.6 11.3 %copy-start.7 = (s32[64,8]{0,1:T(8,128)S(1)}, s32[64,8]{0,1:T(8,128)}, u32[]{:S(2)}) copy-start(s32[64,8]{0,1:T(8,128)} %param.11) | copy-start | bytes 6148
  0.6 12.0 %copy-start.8 = (f32[64,8]{0,1:T(8,128)S(1)}, f32[64,8]{0,1:T(8,128)}, u32[]{:S(2)}) copy-start(f32[64,8]{0,1:T(8,128)} %param.12) | copy-start | bytes 6148
  1.3 1.1 %copy-start = (bf16[32,9216]{1,0:T(8,128)(2,1)S(1)}, bf16[32,9216]{1,0:T(8,128)(2,1)}, u32[]{:S(2)}) copy-start(bf16[32,9216]{1,0:T(8,128)(2,1)} %green.1) | copy-start | bytes 1769476
  2.4 1.1 %copy-start.1 = (bf16[32,9216]{1,0:T(8,128)(2,1)S(1)}, bf16[32,9216]{1,0:T(8,128)(2,1)}, u32[]{:S(2)}) copy-start(bf16[32,9216]{1,0:T(8,128)(2,1)} %sigma_in.1) | copy-start | bytes 1769476
  8.7 5.7 %collective-permute-start = (bf16[16,4608]{1,0:T(8,128)(2,1)S(1)}, bf16[16,4608]{1,0:T(8,128)(2,1)S(1)}, u32[]{:S(2)}, u32[]{:S(2)}) collective-permute-start(bf16[16,4608]{1,0:T(8,128)(2,1)S(1)} %get-tuple-element.10), channel_id=1, source_target_pairs={{0,1},{1,0},{2,3},{3,2},{4,5},{5,4},{6,7},{7,6},{8,9},{9,8},{10,11... | collective-permute-start | bytes 442376 | tf_op jit(solution)/shard_map/ppermute | solution.py:205
  10.1 7.2 %collective-permute-start.1 = (bf16[16,4608]{1,0:T(8,128)(2,1)S(1)}, bf16[16,4608]{1,0:T(8,128)(2,1)S(1)}, u32[]{:S(2)}, u32[]{:S(2)}) collective-permute-start(bf16[16,4608]{1,0:T(8,128)(2,1)S(1)} %get-tuple-element.11), channel_id=1, source_target_pairs={{1,2},{2,1},{5,6},{6,5},{9,10},{10,9},{13,14},{14,13},{17,18},{18,... | collective-permute-start | bytes 442376 | tf_op jit(solution)/shard_map/ppermute | solution.py:205
  17.3 0.8 %copy-start.2 = (s32[64,8]{1,0:T(8,128)S(1)}, s32[64,8]{1,0:T(8,128)}, u32[]{:S(2)}) copy-start(s32[64,8]{1,0:T(8,128)} %copy.11.neighbours) | copy-start | bytes 6148
  18.0 0.8 %copy-start.3 = (f32[64,8]{1,0:T(8,128)S(1)}, f32[64,8]{1,0:T(8,128)}, u32[]{:S(2)}) copy-start(f32[64,8]{1,0:T(8,128)} %copy.12.coupling) | copy-start | bytes 6148
  19.5 14.5 %collective-permute-start.3 = (bf16[64,4608]{1,0:T(8,128)(2,1)S(1)}, bf16[64,4608]{1,0:T(8,128)(2,1)S(1)}, u32[]{:S(2)}, u32[]{:S(2)}) collective-permute-start(bf16[64,4608]{1,0:T(8,128)(2,1)S(1)} %shard_map.105.here), channel_id=1, source_target_pairs={{4,8},{8,4},{12,16},{16,12},{20,24},{24,20},{28,32},{32,28},{36,40... | collective-permute-start | bytes 1769480 | tf_op jit(solution)/shard_map/ppermute | solution.py:205
  22.0 12.1 %collective-permute-start.2 = (bf16[64,4608]{1,0:T(8,128)(2,1)S(1)}, bf16[64,4608]{1,0:T(8,128)(2,1)}, u32[]{:S(2)}, u32[]{:S(2)}) collective-permute-start(bf16[64,4608]{1,0:T(8,128)(2,1)S(1)} %shard_map.105.here), channel_id=1, source_target_pairs={{0,4},{4,0},{8,12},{12,8},{16,20},{20,16},{24,28},{28,24},{32,36},... | collective-permute-start | bytes 1769480 | tf_op jit(solution)/shard_map/ppermute | solution.py:205
  23.1 12.1 %copy-start.4 = (s32[16]{0:T(128)S(1)}, s32[16]{0:T(128)}, u32[]{:S(2)}) copy-start(s32[16]{0:T(128)} %offsets.1) | copy-start | bytes 196
  23.1 12.1 %copy-start.5 = (f32[16]{0:T(128)S(1)}, f32[16]{0:T(128)}, u32[]{:S(2)}) copy-start(f32[16]{0:T(128)} %w_emit.1) | copy-start | bytes 196
  23.1 12.1 %copy-start.6 = (f32[16]{0:T(128)S(1)}, f32[16]{0:T(128)}, u32[]{:S(2)}) copy-start(f32[16]{0:T(128)} %w_absorb.1) | copy-start | bytes 196
where the time goes:
time: 43.6 us; the launch traced here: 43.1 us
  waiting for transfers between devices  14.8 us (34%)
  Pallas kernels  13.8 us (32%)
  starting transfers between devices  6.88 us (16%)
  local copies, waits for them, and re-layouts  5.05 us (12%)
  other arithmetic  1.85 us (4%)
  between operations  0.75 us (2%)
    ppermute x4, waiting for transfers between devices, swap(): return lax.ppermute(block, axis, pairs)  14.8 us
    pallas_call x1, Pallas kernels, on_device(): pl.pallas_call(final_kernel, out_shape=(flat, flat), in_specs=smem(3) + v...  7.9 us
    ppermute x4, starting transfers between devices, swap(): return lax.ppermute(block, axis, pairs)  6.88 us
    pallas_call x1, Pallas kernels, on_device(): pl.pallas_call(lesser_kernel, out_shape=(whole, whole, block, edge, edge)...  5.21 us
    unnamed x20, local copies, waits for them, and re-layouts  5.05 us
    select_n x1, other arithmetic, on_device(): after = jnp.where(odd_energy, apart, beside)  1.15 us
  transfers between devices with their start and end apart: 4, of which 3 were waited for; matrix products, arithmetic and copies ran while one was open for 3% of the time, Pallas kernels for 0%

commit v1 on v0

v1 whole, which is shorter than its diff:
```python
import jax
import jax.numpy as jnp
from jax import lax
from jax.experimental import pallas as pl
from jax.experimental.pallas import tpu as pltpu
from jax.sharding import PartitionSpec as P

ORB = 12
PAIRS = 144
NBRS = 8
FREQS = 16
LANES = 128
GROUPS = 4
ROWS = 32
ATOMS = 64
EDGE = 16
NEAR = 16
SPAN = NEAR * PAIRS
TILES = SPAN // LANES
QUADS = PAIRS // GROUPS
WIDTH = PAIRS * ROWS
WIDE = 512
BATCH = 12
F32 = jnp.float32
BF16 = jnp.bfloat16


def lane_iota(shape):
    return lax.broadcasted_iota(jnp.int32, shape, len(shape) - 1)


def row_iota(shape):
    return lax.broadcasted_iota(jnp.int32, shape, len(shape) - 2)


def identity(size):
    return (lane_iota((size, size)) == row_iota((size, size))).astype(BF16)


def matmul(lhs, rhs):
    return jnp.dot(lhs, rhs, preferred_element_type=F32)


def matmul_first(lhs, rhs):
    return lax.dot_general(lhs, rhs, (((0,), (0,)), ((), ())), preferred_element_type=F32)


def flip(eye, tile):
    return lax.dot_general(eye, tile, (((1,), (1,)), ((), ())), preferred_element_type=F32)


def to_batch_lanes(source, flat, target):
    eye = identity(LANES)
    for t in range(TILES):
        columns = [source[:, h * SPAN + t * LANES : h * SPAN + (t + 1) * LANES] for h in range(GROUPS)]
        flat[t * LANES : (t + 1) * LANES, :] = flip(eye, jnp.concatenate(columns, axis=0))
    for p in range(PAIRS):
        for g in range(2):
            target[p, 8 * g : 8 * g + 8, :] = flat[pl.ds(8 * g * PAIRS + p, 8, stride=PAIRS), :]


def to_energy_rows(flat, target, half):
    eye = identity(LANES)
    for t in range(half * TILES // 2, (half + 1) * TILES // 2):
        turned = flip(eye, flat[t * LANES : (t + 1) * LANES, :].astype(BF16)).astype(BF16)
        for h in range(GROUPS):
            column = h * SPAN + t * LANES
            target[:, column : column + LANES] = turned[h * ROWS : (h + 1) * ROWS]


def send_half(source, target, semaphores, half):
    copies = []
    for h in range(GROUPS):
        columns = pl.ds(h * SPAN + half * SPAN // 2, SPAN // 2)
        copy = pltpu.make_async_copy(source.at[:, columns], target.at[:, columns], semaphores.at[half * GROUPS + h])
        copy.start()
        copies.append(copy)
    return copies


def sandwich_half(left, middle, g, store):
    depth = 3
    half = slice(8 * g, 8 * g + 8)

    def body(step, carry):
        first = step * depth
        product = [[None] * ORB for _ in range(depth)]
        for j in range(ORB):
            lhs = [left[(first + r) * ORB + j, half, :] for r in range(depth)]
            for k in range(ORB):
                rhs = middle[j * ORB + k, half, :]
                for r in range(depth):
                    term = lhs[r] * rhs
                    product[r][k] = term if j == 0 else product[r][k] + term
        for l in range(ORB):
            total = [None] * depth
            for k in range(ORB):
                rhs = left[l * ORB + k, half, :]
                for r in range(depth):
                    term = product[r][k] * rhs
                    total[r] = term if k == 0 else total[r] + term
            for r in range(depth):
                store((first + r) * ORB + l, half, total[r])
        return carry

    lax.fori_loop(0, ORB // depth, body, 0)


def chunk_swap():
    distance = lane_iota((LANES, LANES)) - row_iota((LANES, LANES))
    group = row_iota((LANES, LANES)) // ROWS
    rows = []
    for a in range(GROUPS):
        row = [((distance == ROWS * (a - b)) & (group == b)).astype(BF16) for b in range(GROUPS)]
        rows.append(jnp.concatenate(row, axis=1))
    return jnp.concatenate(rows, axis=0)


def band(offsets, w_emit, w_absorb, odd):
    shape = (ROWS, LANES)
    distance = lane_iota(shape) % ROWS - row_iota(shape)
    before = jnp.zeros(shape, F32)
    here = jnp.zeros(shape, F32)
    after = jnp.zeros(shape, F32)
    for w in range(FREQS):
        off, emit, absorb = offsets[w], w_emit[w], w_absorb[w]
        before = before + jnp.where(distance + ROWS == off, emit, 0.0)
        here = here + jnp.where(distance == off, emit, 0.0) + jnp.where(-distance == off, absorb, 0.0)
        after = after + jnp.where(ROWS - distance == off, absorb, 0.0)
    apart = jnp.where(odd, after, before)
    beside = jnp.where(odd, before, after)
    group = lane_iota(shape) // ROWS
    parts = []
    for block in (apart, here, beside):
        parts += [jnp.where(group == h, block, 0.0) for h in range(GROUPS)]
    return jnp.concatenate(parts, axis=0).astype(BF16)


def atom_order(first_hot, second_hot):
    edge = jnp.maximum(jnp.max(first_hot, axis=1, keepdims=True), jnp.max(second_hot, axis=1, keepdims=True))
    shape = (ATOMS, ATOMS)
    earlier = jnp.sum(jnp.where(row_iota(shape) < lane_iota(shape), edge, 0.0), axis=0, keepdims=True)
    itself = jnp.sum(jnp.where(row_iota(shape) == lane_iota(shape), edge, 0.0), axis=0, keepdims=True)
    count = jnp.sum(jnp.broadcast_to(edge, shape), axis=0, keepdims=True)
    number = lane_iota((1, ATOMS)).astype(F32)
    place = jnp.where(itself > 0.5, earlier, count + number - earlier)
    return (row_iota(shape).astype(F32) == place).astype(BF16)


def mixing(neighbours, coupling, order, odd):
    names = row_iota((ATOMS + 2 * EDGE, ATOMS))
    weights = jnp.zeros((ATOMS + 2 * EDGE, ATOMS), F32)
    for k in range(NBRS):
        weights = weights + jnp.where(names == neighbours[k : k + 1, :], coupling[k : k + 1, :], 0.0)
    low, high = weights[ATOMS : ATOMS + EDGE], weights[ATOMS + EDGE :]
    edges = [jnp.where(odd, low, high), jnp.where(odd, high, low)]
    weights = jnp.concatenate([weights[:ATOMS]] + edges, axis=0)
    coarse = weights.astype(BF16)
    fine = (weights - coarse.astype(F32)).astype(BF16)
    rows = []
    for part in (coarse, fine):
        rows += [matmul(order, part[:ATOMS]).astype(BF16), part[ATOMS:]]
    return flip(identity(ATOMS), jnp.concatenate(rows, axis=0)).astype(BF16)


def lesser_kernel(
    green, sigma_in, *rest
):
    small = rest[:7]
    green_t, sigma_t, own, near, far, matrix, weights, pick, swapper = rest[7:16]
    held = rest[16:23]
    green_here, sigma_here, flat, result, grouped, semaphores, small_semaphores = rest[23:]
    copies = []
    fetched = []
    for n, (source, target) in enumerate(zip(small, held)):
        copy = pltpu.make_async_copy(source, target, small_semaphores.at[n])
        copy.start()
        fetched.append(copy)
    for n, (source, target) in enumerate(((green, green_here), (sigma_in, sigma_here))):
        for h in range(GROUPS):
            columns = pl.ds(h * SPAN, SPAN)
            copy = pltpu.make_async_copy(
                source.at[:, columns], target.at[:, columns], semaphores.at[n * GROUPS + h]
            )
            copy.start()
            copies.append(copy)
    swapper[...] = chunk_swap()
    for copy in fetched:
        copy.wait()
    offsets, w_emit, w_absorb, neighbours, coupling, send_down, send_up = held
    odd_slab = lax.axis_index("slab") % 2 == 1
    odd_energy = lax.axis_index("energy") % 2 == 1
    down_hot = (row_iota((ATOMS, EDGE)) == send_down[...]).astype(F32)
    up_hot = (row_iota((ATOMS, EDGE)) == send_up[...]).astype(F32)
    first_hot = jnp.where(odd_slab, down_hot, up_hot)
    second_hot = jnp.where(odd_slab, up_hot, down_hot)
    order = atom_order(first_hot, second_hot)
    hot = jnp.concatenate([first_hot, second_hot], axis=1).astype(BF16)
    pick[...] = matmul(order[: 2 * EDGE], hot).astype(BF16)
    weights[...] = mixing(neighbours, coupling, order, odd_slab)
    matrix[...] = band(offsets, w_emit, w_absorb, odd_energy)
    for copy in copies[:GROUPS]:
        copy.wait()
    to_batch_lanes(green_here, flat, green_t)
    for copy in copies[GROUPS:]:
        copy.wait()
    to_batch_lanes(sigma_here, flat, sigma_t)

    def store(p, half, value):
        result[p, half, :] = value

    for g in range(2):
        sandwich_half(green_t, sigma_t, g, store)
    for base in range(0, QUADS, BATCH):
        columns = []
        for j in range(GROUPS):
            columns.append(jnp.concatenate(
                [result[GROUPS * q + j].astype(BF16) for q in range(base, base + BATCH)], axis=0
            ))
        moved = matmul(jnp.concatenate(columns, axis=1), swapper[...]).astype(BF16)
        for i in range(BATCH):
            for h in range(GROUPS):
                grouped[h * NEAR : (h + 1) * NEAR, (base + i) * LANES : (base + i + 1) * LANES] = moved[
                    i * NEAR : (i + 1) * NEAR, h * LANES : (h + 1) * LANES
                ]
    for t in range(WIDTH // WIDE):
        columns = slice(t * WIDE, (t + 1) * WIDE)
        ordered = matmul(order, grouped[:, columns]).astype(BF16)
        own[:, columns] = ordered
        near[:, columns] = ordered[: 2 * EDGE]
        far[:, columns] = ordered[2 * EDGE :]


def convolve(matrix, apart, here, beside, target):
    for base in range(0, QUADS, BATCH):
        lhs = []
        for source in (apart, here, beside):
            lhs.append(jnp.concatenate(
                [source[:, q * LANES : (q + 1) * LANES] for q in range(base, base + BATCH)], axis=0
            ))
        total = matmul(jnp.concatenate(lhs, axis=1), matrix[...]).astype(BF16)
        for i in range(BATCH):
            column = (base + i) * LANES
            target[:, column : column + LANES] = total[i * 2 * EDGE : (i + 1) * 2 * EDGE]


def near_kernel(matrix, pick, apart, here, beside, target, first, second):
    convolve(matrix, apart, here, beside.at[: 2 * EDGE, :], target)
    for t in range(WIDTH // WIDE):
        columns = slice(t * WIDE, (t + 1) * WIDE)
        picked = matmul_first(pick[...], target[:, columns]).astype(BF16)
        first[:, columns] = picked[:EDGE]
        second[:, columns] = picked[EDGE:]


def far_kernel(matrix, apart, here, beside, target):
    convolve(matrix, apart, here, beside.at[2 * EDGE :, :], target)


def final_kernel(
    weights, swapper, near, far, first, second, green_t, sigma_t, sigma_ph, g_less,
    flat, flat_less, middle, sigma_here, less_here, semaphores, less_semaphores,
):
    for base in range(0, QUADS, BATCH):
        parts = []
        for t in range(base * LANES // WIDE, (base + BATCH) * LANES // WIDE):
            columns = slice(t * WIDE, (t + 1) * WIDE)
            listed = [near[:, columns], far[:, columns], first[:, columns], second[:, columns]]
            extended = jnp.concatenate(listed + listed, axis=0)
            parts.append(matmul(weights[...], extended).astype(BF16))
        mixed = jnp.concatenate(parts, axis=1)
        columns = []
        for h in range(GROUPS):
            columns.append(jnp.concatenate(
                [mixed[h * NEAR : (h + 1) * NEAR, i * LANES : (i + 1) * LANES] for i in range(BATCH)], axis=0
            ))
        moved = matmul(jnp.concatenate(columns, axis=1), swapper[...])
        for i in range(BATCH):
            for j in range(GROUPS):
                p = GROUPS * (base + i) + j
                part = moved[i * NEAR : (i + 1) * NEAR, j * LANES : (j + 1) * LANES]
                middle[p] = sigma_t[p] + part
                for g in range(2):
                    flat[pl.ds(8 * g * PAIRS + p, 8, stride=PAIRS), :] = part[8 * g : 8 * g + 8]
    copies = []
    for g in range(2):
        to_energy_rows(flat, sigma_here, g)
        copies += send_half(sigma_here, sigma_ph, semaphores, g)

    for g in range(2):
        def store(p, half, value):
            flat_less[pl.ds(8 * g * PAIRS + p, 8, stride=PAIRS), :] = value

        sandwich_half(green_t, middle, g, store)
        to_energy_rows(flat_less, less_here, g)
        copies += send_half(less_here, g_less, less_semaphores, g)
    for copy in copies:
        copy.wait()


def vmem(count):
    return [pl.BlockSpec(memory_space=pltpu.VMEM)] * count


def anywhere(count):
    return [pl.BlockSpec(memory_space=pl.ANY)] * count


PARAMS = pltpu.CompilerParams(vmem_limit_bytes=44 * 1024 * 1024)


def swap(block, axis, parity):
    pairs = []
    for i in range(parity, lax.axis_size(axis) - 1, 2):
        pairs += [(i, i + 1), (i + 1, i)]
    return lax.ppermute(block, axis, pairs)


def shape_of(*shape, kind=BF16):
    return jax.ShapeDtypeStruct(shape, kind)


def on_device(green, sigma_in, neighbours, coupling, send_down, send_up, offsets, w_emit, w_absorb):
    whole = shape_of(PAIRS, NEAR, LANES, kind=F32)
    half = shape_of(2 * EDGE, WIDTH)
    edge = shape_of(EDGE, WIDTH)
    given = (green, sigma_in, offsets, w_emit, w_absorb, neighbours.T, coupling.T, send_down, send_up)
    given = [pltpu.with_memory_space_constraint(array, pltpu.HBM) for array in given]
    green_t, sigma_t, own, near, far, matrix, weights, pick, swapper = pl.pallas_call(
        lesser_kernel,
        out_shape=(
            whole, whole, shape_of(ATOMS, WIDTH), half, half, shape_of(3 * LANES, LANES),
            shape_of(ATOMS, 2 * (ATOMS + 2 * EDGE)), shape_of(2 * EDGE, 2 * EDGE), shape_of(WIDE, WIDE),
        ),
        in_specs=anywhere(9),
        out_specs=tuple(vmem(9)),
        scratch_shapes=[
            pltpu.SMEM((FREQS,), jnp.int32),
            pltpu.SMEM((FREQS,), F32),
            pltpu.SMEM((FREQS,), F32),
            pltpu.VMEM((NBRS, ATOMS), jnp.int32),
            pltpu.VMEM((NBRS, ATOMS), F32),
            pltpu.VMEM((1, EDGE), jnp.int32),
            pltpu.VMEM((1, EDGE), jnp.int32),
            pltpu.VMEM((ROWS, ATOMS * PAIRS), BF16),
            pltpu.VMEM((ROWS, ATOMS * PAIRS), BF16),
            pltpu.VMEM((SPAN, LANES), F32),
            pltpu.VMEM((PAIRS, NEAR, LANES), F32),
            pltpu.VMEM((ATOMS, WIDTH), BF16),
            pltpu.SemaphoreType.DMA((2 * GROUPS,)),
            pltpu.SemaphoreType.DMA((7,)),
        ],
        compiler_params=PARAMS,
    )(*given)
    near_apart = swap(near, "energy", 1)
    far_apart = swap(far, "energy", 1)
    beside = swap(own, "energy", 0)
    near_done, first, second = pl.pallas_call(
        near_kernel,
        out_shape=(half, edge, edge),
        in_specs=vmem(5),
        out_specs=tuple(vmem(3)),
        compiler_params=PARAMS,
    )(matrix, pick, near_apart, near, beside)
    first = swap(first, "slab", 0)
    second = swap(second, "slab", 1)
    far_done = pl.pallas_call(
        far_kernel,
        out_shape=half,
        in_specs=vmem(4),
        out_specs=vmem(1)[0],
        compiler_params=PARAMS,
    )(matrix, far_apart, far, beside)
    flat = shape_of(ROWS, ATOMS * PAIRS)
    return pl.pallas_call(
        final_kernel,
        out_shape=(flat, flat),
        in_specs=vmem(8),
        out_specs=tuple(anywhere(2)),
        scratch_shapes=[
            pltpu.VMEM((SPAN, LANES), F32),
            pltpu.VMEM((SPAN, LANES), F32),
            pltpu.VMEM((PAIRS, NEAR, LANES), F32),
            pltpu.VMEM((ROWS, ATOMS * PAIRS), BF16),
            pltpu.VMEM((ROWS, ATOMS * PAIRS), BF16),
            pltpu.SemaphoreType.DMA((2 * GROUPS,)),
            pltpu.SemaphoreType.DMA((2 * GROUPS,)),
        ],
        compiler_params=PARAMS,
    )(weights, swapper, near_done, far_done, first, second, green_t, sigma_t)


def solution(mesh):
    split = P("energy", "slab")
    by_slab = P("slab", None)
    return jax.shard_map(
        on_device,
        mesh=mesh,
        in_specs=(split, split, by_slab, by_slab, by_slab, by_slab, P(), P(), P()),
        out_specs=(split, split),
        check_vma=False,
    )
```

time: 43.6 us -> 32.7 us (0.75)
  waiting for transfers between devices: 14.8 us -> 7.18 us
  starting transfers between devices: 6.88 us -> 12.3 us
  local copies, waits for them, and re-layouts: 5.05 us -> 0 us
  other arithmetic: 1.85 us -> 0 us
  Pallas kernels: 13.8 us -> 12.4 us
    ppermute x4 -> x5, waiting for transfers between devices: 14.8 us -> 7.18 us  [swap(): return lax.ppermute(block, axis, pairs)]
    ppermute x4 -> x5, starting transfers between devices: 6.88 us -> 12.3 us  [swap(): return lax.ppermute(block, axis, pairs)]
    unnamed x20 -> x0, local copies, waits for them, and re-layouts: 5.05 us -> none
    select_n x3 -> x0, other arithmetic: 1.85 us -> none  [the longest x1 1.15 us: on_device(): after = jnp.where(odd_energy, apart, beside)]
    pallas_call x3 -> x4, Pallas kernels: 13.8 us -> 12.4 us  [the longest x1 6.13 us: on_device(): pl.pallas_call(lesser_kernel, out_shape=(whole, whole, shape_of(ATOMS, WI...]
  transfers between devices with their start and end apart: 4 -> 5, of which waited for: 3 -> 4; matrix products, arithmetic and copies ran while one was open for 3% -> 0% of each run, Pallas kernels for 0% -> 3%
where the time goes in v1:
time: 32.7 us; the launch traced here: 32.6 us
  Pallas kernels  12.4 us (38%)
  starting transfers between devices  12.3 us (38%)
  waiting for transfers between devices  7.18 us (22%)
  between operations  0.68 us (2%)
    ppermute x5, starting transfers between devices, swap(): return lax.ppermute(block, axis, pairs)  12.3 us
    ppermute x5, waiting for transfers between devices, swap(): return lax.ppermute(block, axis, pairs)  7.18 us
    pallas_call x1, Pallas kernels, on_device(): pl.pallas_call(lesser_kernel, out_shape=(whole, whole, shape_of(ATOMS, WI...  6.13 us
    pallas_call x1, Pallas kernels, on_device(): pl.pallas_call(final_kernel, out_shape=(flat, flat), in_specs=vmem(8), ou...  5.35 us
  transfers between devices with their start and end apart: 5, of which 4 were waited for; matrix products, arithmetic and copies ran while one was open for 0% of the time, Pallas kernels for 3%

profile of v1, /device:TPU:144, one launch (start us, length us, event | category | flops | bytes accessed | tf_op | source)
XLA Modules:
  0.0 32.6 jit_solution(3416588032466652252)
XLA Ops:
  0.6 6.1 %shard_map.104 = (f32[144,16,128]{2,1,0:T(8,128)S(1)}, f32[144,16,128]{2,1,0:T(8,128)S(1)}, bf16[64,4608]{1,0:T(8,128)(2,1)S(1)}, bf16[32,4608]{1,0:T(8,128)(2,1...) custom-call(bf16[32,9216]{1,0:T(8,128)(2,1)} %green.1, ...), custom_call_target="tpu_custom_call" | custom-call | tf_op jit(solution)/shard_map/pallas_call | solution.py:329
  6.8 0.1 collective-permute-start.1
  6.9 4.3 %collective-permute-start = (bf16[32,4608]{1,0:T(8,128)(2,1)S(1)}, bf16[32,4608]{1,0:T(8,128)(2,1)S(1)}, u32[]{:S(2)}, u32[]{:S(2)}) collective-permute-start(bf16[32,4608]{1,0:T(8,128)(2,1)S(1)} %get-tuple-element.18.here), channel_id=1, source_target_pairs={{4,8},{8,4},{12,16},{16,12},{20,24},{24,20},{28,32},{32,28},{36,40... | collective-permute-start | bytes 884744 | tf_op jit(solution)/shard_map/ppermute | solution.py:316
  11.2 4.6 %collective-permute-start.2 = (bf16[32,4608]{1,0:T(8,128)(2,1)S(1)}, bf16[32,4608]{1,0:T(8,128)(2,1)S(1)}, u32[]{:S(2)}, u32[]{:S(2)}) collective-permute-start(bf16[32,4608]{1,0:T(8,128)(2,1)S(1)} %get-tuple-element.21.here), channel_id=1, source_target_pairs={{4,8},{8,4},{12,16},{16,12},{20,24},{24,20},{28,32},{32,28},{36,40... | collective-permute-start | bytes 884744 | tf_op jit(solution)/shard_map/ppermute | solution.py:316
  15.8 2.5 %collective-permute-done.apart = bf16[32,4608]{1,0:T(8,128)(2,1)S(1)} collective-permute-done((bf16[32,4608]{1,0:T(8,128)(2,1)S(1)}, bf16[32,4608]{1,0:T(8,128)(2,1)S(1)}, u32[]{:S(2)}, u32[]{:S(2)}) %collective-permute-start) | collective-permute-done | bytes 294944 | tf_op jit(solution)/shard_map/ppermute | solution.py:316
  18.2 0.0 collective-permute-done.1.beside
  18.2 0.6 %shard_map.105 = (bf16[32,4608]{1,0:T(8,128)(2,1)S(1)}, bf16[16,4608]{1,0:T(8,128)(2,1)S(1)}, bf16[16,4608]{1,0:T(8,128)(2,1)S(1)}) custom-call(bf16[384,128]{1,0:T(8,128)(2,1)S(1)} %get-tuple-element.16.matrix, bf16[32,32]{1,0:T(8,128)(2,1)S(1)} %get-tuple-element.17.pick, bf16[32,4608]{1,0:T(8,128)(2,1)S(1)} %collective-permute-done.apart, ...), custom_call_target="tpu_custom_call" | custom-call | tf_op jit(solution)/shard_map/pallas_call | solution.py:358
  18.8 1.4 %collective-permute-start.3 = (bf16[16,4608]{1,0:T(8,128)(2,1)S(1)}, bf16[16,4608]{1,0:T(8,128)(2,1)S(1)}, u32[]{:S(2)}, u32[]{:S(2)}) collective-permute-start(bf16[16,4608]{1,0:T(8,128)(2,1)S(1)} %get-tuple-element.22), channel_id=1, source_target_pairs={{0,1},{1,0},{2,3},{3,2},{4,5},{5,4},{6,7},{7,6},{8,9},{9,8},{10,11... | collective-permute-start | bytes 442376 | tf_op jit(solution)/shard_map/ppermute | solution.py:316
  20.2 1.9 %collective-permute-start.4 = (bf16[16,4608]{1,0:T(8,128)(2,1)S(1)}, bf16[16,4608]{1,0:T(8,128)(2,1)S(1)}, u32[]{:S(2)}, u32[]{:S(2)}) collective-permute-start(bf16[16,4608]{1,0:T(8,128)(2,1)S(1)} %get-tuple-element.23), channel_id=1, source_target_pairs={{1,2},{2,1},{5,6},{6,5},{9,10},{10,9},{13,14},{14,13},{17,18},{18,... | collective-permute-start | bytes 442376 | tf_op jit(solution)/shard_map/ppermute | solution.py:316
  22.1 0.5 %collective-permute-done.2.apart = bf16[32,4608]{1,0:T(8,128)(2,1)S(1)} collective-permute-done((bf16[32,4608]{1,0:T(8,128)(2,1)S(1)}, bf16[32,4608]{1,0:T(8,128)(2,1)S(1)}, u32[]{:S(2)}, u32[]{:S(2)}) %collective-permute-start.2) | collective-permute-done | bytes 294944 | tf_op jit(solution)/shard_map/ppermute | solution.py:316
  22.5 0.4 %shard_map.106.far = bf16[32,4608]{1,0:T(8,128)(2,1)S(1)} custom-call(bf16[384,128]{1,0:T(8,128)(2,1)S(1)} %get-tuple-element.16.matrix, bf16[32,4608]{1,0:T(8,128)(2,1)S(1)} %collective-permute-done.2.apart, bf16[32,4608]{1,0:T(8,128)(2,1)S(1)} %get-tuple-element.21.here, bf16[64,4608]{1,0:T(8,128)(2,1)S(1)} %collective-permute-done.1.beside), custom_call_target="tpu_custom_call" | custom-call | tf_op jit(solution)/shard_map/pallas_call | solution.py:367
  22.9 1.1 %collective-permute-done.3.first = bf16[16,4608]{1,0:T(8,128)(2,1)S(1)} collective-permute-done((bf16[16,4608]{1,0:T(8,128)(2,1)S(1)}, bf16[16,4608]{1,0:T(8,128)(2,1)S(1)}, u32[]{:S(2)}, u32[]{:S(2)}) %collective-permute-start.3) | collective-permute-done | bytes 147488 | tf_op jit(solution)/shard_map/ppermute | solution.py:316
  24.0 3.2 %collective-permute-done.4.second = bf16[16,4608]{1,0:T(8,128)(2,1)S(1)} collective-permute-done((bf16[16,4608]{1,0:T(8,128)(2,1)S(1)}, bf16[16,4608]{1,0:T(8,128)(2,1)S(1)}, u32[]{:S(2)}, u32[]{:S(2)}) %collective-permute-start.4) | collective-permute-done | bytes 147488 | tf_op jit(solution)/shard_map/ppermute | solution.py:316
  27.2 5.4 %shard_map.107 = (bf16[32,9216]{1,0:T(8,128)(2,1)}, bf16[32,9216]{1,0:T(8,128)(2,1)}) custom-call(bf16[64,192]{1,0:T(8,128)(2,1)S(1)} %get-tuple-element.14.weights, bf16[512,512]{1,0:T(8,128)(2,1)S(1)} %get-tuple-element.15.swapper, bf16[32,4608]{1,0:T(8,128)(2,1)S(1)} %get-tuple-element.20.near, bf16[32,4608]{1,0:T(8,128)(2,1)S(1)} %shard_map.106.far, ...), custom_call_target="tpu_custom_call" | custom-call | tf_op jit(solution)/shard_map/pallas_call | solution.py:375
Async XLA Ops:
  6.8 11.5 %collective-permute-start.1 = (bf16[64,4608]{1,0:T(8,128)(2,1)S(1)}, bf16[64,4608]{1,0:T(8,128)(2,1)S(1)}, u32[]{:S(2)}, u32[]{:S(2)}) collective-permute-start(bf16[64,4608]{1,0:T(8,128)(2,1)S(1)} %get-tuple-element.19), channel_id=1, source_target_pairs={{0,4},{4,0},{8,12},{12,8},{16,20},{20,16},{24,28},{28,24},{32,36},... | collective-permute-start | bytes 1769480 | tf_op jit(solution)/shard_map/ppermute | solution.py:316
  6.9 11.4 %collective-permute-start = (bf16[32,4608]{1,0:T(8,128)(2,1)S(1)}, bf16[32,4608]{1,0:T(8,128)(2,1)S(1)}, u32[]{:S(2)}, u32[]{:S(2)}) collective-permute-start(bf16[32,4608]{1,0:T(8,128)(2,1)S(1)} %get-tuple-element.18.here), channel_id=1, source_target_pairs={{4,8},{8,4},{12,16},{16,12},{20,24},{24,20},{28,32},{32,28},{36,40... | collective-permute-start | bytes 884744 | tf_op jit(solution)/shard_map/ppermute | solution.py:316
  11.2 11.4 %collective-permute-start.2 = (bf16[32,4608]{1,0:T(8,128)(2,1)S(1)}, bf16[32,4608]{1,0:T(8,128)(2,1)S(1)}, u32[]{:S(2)}, u32[]{:S(2)}) collective-permute-start(bf16[32,4608]{1,0:T(8,128)(2,1)S(1)} %get-tuple-element.21.here), channel_id=1, source_target_pairs={{4,8},{8,4},{12,16},{16,12},{20,24},{24,20},{28,32},{32,28},{36,40... | collective-permute-start | bytes 884744 | tf_op jit(solution)/shard_map/ppermute | solution.py:316
  18.8 5.2 %collective-permute-start.3 = (bf16[16,4608]{1,0:T(8,128)(2,1)S(1)}, bf16[16,4608]{1,0:T(8,128)(2,1)S(1)}, u32[]{:S(2)}, u32[]{:S(2)}) collective-permute-start(bf16[16,4608]{1,0:T(8,128)(2,1)S(1)} %get-tuple-element.22), channel_id=1, source_target_pairs={{0,1},{1,0},{2,3},{3,2},{4,5},{5,4},{6,7},{7,6},{8,9},{9,8},{10,11... | collective-permute-start | bytes 442376 | tf_op jit(solution)/shard_map/ppermute | solution.py:316
  20.2 7.0 %collective-permute-start.4 = (bf16[16,4608]{1,0:T(8,128)(2,1)S(1)}, bf16[16,4608]{1,0:T(8,128)(2,1)S(1)}, u32[]{:S(2)}, u32[]{:S(2)}) collective-permute-start(bf16[16,4608]{1,0:T(8,128)(2,1)S(1)} %get-tuple-element.23), channel_id=1, source_target_pairs={{1,2},{2,1},{5,6},{6,5},{9,10},{10,9},{13,14},{14,13},{17,18},{18,... | collective-permute-start | bytes 442376 | tf_op jit(solution)/shard_map/ppermute | solution.py:316

commit v2 on v1

--- a/solution.py
+++ b/solution.py
@@ -16,6 +16,7 @@
 EDGE = 16
 NEAR = 16
 SPAN = NEAR * PAIRS
+PITCH = PAIRS + 1
 TILES = SPAN // LANES
 QUADS = PAIRS // GROUPS
 WIDTH = PAIRS * ROWS
@@ -49,26 +50,37 @@
     return lax.dot_general(eye, tile, (((1,), (1,)), ((), ())), preferred_element_type=F32)
 
 
-def to_batch_lanes(source, flat, target):
-    eye = identity(LANES)
-    for t in range(TILES):
+def pieces(t):
+    row, stop = t * LANES, (t + 1) * LANES
+    while row < stop:
+        atom = row // PAIRS
+        size = min(stop, (atom + 1) * PAIRS) - row
+        yield row - t * LANES, row + atom * (PITCH - PAIRS), size
+        row += size
+
+
+def atom_rows(p, g):
+    return pl.ds(8 * g * PITCH + p, 8, stride=PITCH)
+
+
+def to_batch_lanes(source, target, half):
+    for t in range(half * TILES // 2, (half + 1) * TILES // 2):
         columns = [source[:, h * SPAN + t * LANES : h * SPAN + (t + 1) * LANES] for h in range(GROUPS)]
-        flat[t * LANES : (t + 1) * LANES, :] = flip(eye, jnp.concatenate(columns, axis=0))
-    for p in range(PAIRS):
-        for g in range(2):
-            target[p, 8 * g : 8 * g + 8, :] = flat[pl.ds(8 * g * PAIRS + p, 8, stride=PAIRS), :]
+        turned = jnp.concatenate(columns, axis=0).T.astype(F32)
+        for start, row, size in pieces(t):
+            target[row : row + size, :] = turned[start : start + size]
 
 
 def to_energy_rows(flat, target, half):
-    eye = identity(LANES)
     for t in range(half * TILES // 2, (half + 1) * TILES // 2):
-        turned = flip(eye, flat[t * LANES : (t + 1) * LANES, :].astype(BF16)).astype(BF16)
+        rows = [flat[row : row + size, :].astype(BF16) for _, row, size in pieces(t)]
+        turned = jnp.concatenate(rows, axis=0).T
         for h in range(GROUPS):
             column = h * SPAN + t * LANES
             target[:, column : column + LANES] = turned[h * ROWS : (h + 1) * ROWS]
 
 
-def send_half(source, target, semaphores, half):
+def move_half(source, target, semaphores, half):
     copies = []
     for h in range(GROUPS):
         columns = pl.ds(h * SPAN + half * SPAN // 2, SPAN // 2)
@@ -80,27 +92,25 @@
 
 def sandwich_half(left, middle, g, store):
     depth = 3
-    half = slice(8 * g, 8 * g + 8)
-
     def body(step, carry):
         first = step * depth
         product = [[None] * ORB for _ in range(depth)]
         for j in range(ORB):
-            lhs = [left[(first + r) * ORB + j, half, :] for r in range(depth)]
+            lhs = [left[atom_rows((first + r) * ORB + j, g), :] for r in range(depth)]
             for k in range(ORB):
-                rhs = middle[j * ORB + k, half, :]
+                rhs = middle[atom_rows(j * ORB + k, g), :]
                 for r in range(depth):
                     term = lhs[r] * rhs
                     product[r][k] = term if j == 0 else product[r][k] + term
         for l in range(ORB):
             total = [None] * depth
             for k in range(ORB):
-                rhs = left[l * ORB + k, half, :]
+                rhs = left[atom_rows(l * ORB + k, g), :]
                 for r in range(depth):
                     term = product[r][k] * rhs
                     total[r] = term if k == 0 else total[r] + term
             for r in range(depth):
-                store((first + r) * ORB + l, half, total[r])
+                store((first + r) * ORB + l, total[r])
         return carry
 
     lax.fori_loop(0, ORB // depth, body, 0)
@@ -157,33 +167,26 @@
     weights = jnp.concatenate([weights[:ATOMS]] + edges, axis=0)
     coarse = weights.astype(BF16)
     fine = (weights - coarse.astype(F32)).astype(BF16)
-    rows = []
-    for part in (coarse, fine):
-        rows += [matmul(order, part[:ATOMS]).astype(BF16), part[ATOMS:]]
-    return flip(identity(ATOMS), jnp.concatenate(rows, axis=0)).astype(BF16)
+    own = [matmul(order, part[:ATOMS]).astype(BF16) for part in (coarse, fine)]
+    edge = [part[ATOMS:] for part in (coarse, fine)]
+    return [flip(identity(ATOMS), jnp.concatenate(rows, axis=0)).astype(BF16) for rows in (own, edge)]
 
 
 def lesser_kernel(
     green, sigma_in, *rest
 ):
     small = rest[:7]
-    green_t, sigma_t, own, near, far, matrix, weights, pick, swapper = rest[7:16]
+    green_t, sigma_t, near, far, matrix, own_weights, edge_weights, pick, swapper = rest[7:16]
     held = rest[16:23]
-    green_here, sigma_here, flat, result, grouped, semaphores, small_semaphores = rest[23:]
+    green_here, sigma_here, result, grouped, green_semaphores, sigma_semaphores, small_semaphores = rest[23:]
     copies = []
     fetched = []
     for n, (source, target) in enumerate(zip(small, held)):
         copy = pltpu.make_async_copy(source, target, small_semaphores.at[n])
         copy.start()
         fetched.append(copy)
-    for n, (source, target) in enumerate(((green, green_here), (sigma_in, sigma_here))):
-        for h in range(GROUPS):
-            columns = pl.ds(h * SPAN, SPAN)
-            copy = pltpu.make_async_copy(
-                source.at[:, columns], target.at[:, columns], semaphores.at[n * GROUPS + h]
-            )
-            copy.start()
-            copies.append(copy)
+    for source, target, semaphores in ((green, green_here, green_semaphores), (sigma_in, sigma_here, sigma_semaphores)):
+        copies += [move_half(source, target, semaphores, g) for g in range(2)]
     swapper[...] = chunk_swap()
     for copy in fetched:
         copy.wait()
@@ -197,19 +200,17 @@
     order = atom_order(first_hot, second_hot)
     hot = jnp.concatenate([first_hot, second_hot], axis=1).astype(BF16)
     pick[...] = matmul(order[: 2 * EDGE], hot).astype(BF16)
-    weights[...] = mixing(neighbours, coupling, order, odd_slab)
+    own_weights[...], edge_weights[...] = mixing(neighbours, coupling, order, odd_slab)
     matrix[...] = band(offsets, w_emit, w_absorb, odd_energy)
-    for copy in copies[:GROUPS]:
-        copy.wait()
-    to_batch_lanes(green_here, flat, green_t)
-    for copy in copies[GROUPS:]:
-        copy.wait()
-    to_batch_lanes(sigma_here, flat, sigma_t)
-
-    def store(p, half, value):
-        result[p, half, :] = value
-
+    for n, (source, target) in enumerate(((green_here, green_t), (sigma_here, sigma_t))):
+        for g in range(2):
+            for copy in copies[2 * n + g]:
+                copy.wait()
+            to_batch_lanes(source, target, g)
     for g in range(2):
+        def store(p, value):
+            result[p, 8 * g : 8 * g + 8, :] = value
+
         sandwich_half(green_t, sigma_t, g, store)
     for base in range(0, QUADS, BATCH):
         columns = []
@@ -226,7 +227,6 @@
     for t in range(WIDTH // WIDE):
         columns = slice(t * WIDE, (t + 1) * WIDE)
         ordered = matmul(order, grouped[:, columns]).astype(BF16)
-        own[:, columns] = ordered
         near[:, columns] = ordered[: 2 * EDGE]
         far[:, columns] = ordered[2 * EDGE :]
 
@@ -245,7 +245,7 @@
 
 
 def near_kernel(matrix, pick, apart, here, beside, target, first, second):
-    convolve(matrix, apart, here, beside.at[: 2 * EDGE, :], target)
+    convolve(matrix, apart, here, beside, target)
     for t in range(WIDTH // WIDE):
         columns = slice(t * WIDE, (t + 1) * WIDE)
         picked = matmul_first(pick[...], target[:, columns]).astype(BF16)
@@ -253,21 +253,25 @@
         second[:, columns] = picked[EDGE:]
 
 
-def far_kernel(matrix, apart, here, beside, target):
-    convolve(matrix, apart, here, beside.at[2 * EDGE :, :], target)
+def far_kernel(matrix, weights, near, apart, here, beside, mixed, target):
+    convolve(matrix, apart, here, beside, target)
+    for t in range(WIDTH // WIDE):
+        columns = slice(t * WIDE, (t + 1) * WIDE)
+        listed = [near[:, columns], target[:, columns]]
+        mixed[:, columns] = matmul(weights[...], jnp.concatenate(listed + listed, axis=0))
 
 
 def final_kernel(
-    weights, swapper, near, far, first, second, green_t, sigma_t, sigma_ph, g_less,
+    weights, swapper, own, first, second, green_t, sigma_t, sigma_ph, g_less,
     flat, flat_less, middle, sigma_here, less_here, semaphores, less_semaphores,
 ):
     for base in range(0, QUADS, BATCH):
         parts = []
         for t in range(base * LANES // WIDE, (base + BATCH) * LANES // WIDE):
             columns = slice(t * WIDE, (t + 1) * WIDE)
-            listed = [near[:, columns], far[:, columns], first[:, columns], second[:, columns]]
-            extended = jnp.concatenate(listed + listed, axis=0)
-            parts.append(matmul(weights[...], extended).astype(BF16))
+            listed = [first[:, columns], second[:, columns]]
+            edges = matmul(weights[...], jnp.concatenate(listed + listed, axis=0))
+            parts.append((own[:, columns] + edges).astype(BF16))
         mixed = jnp.concatenate(parts, axis=1)
         columns = []
         for h in range(GROUPS):
@@ -277,23 +281,23 @@
         moved = matmul(jnp.concatenate(columns, axis=1), swapper[...])
         for i in range(BATCH):
             for j in range(GROUPS):
-                p = GROUPS * (base + i) + j
                 part = moved[i * NEAR : (i + 1) * NEAR, j * LANES : (j + 1) * LANES]
-                middle[p] = sigma_t[p] + part
                 for g in range(2):
-                    flat[pl.ds(8 * g * PAIRS + p, 8, stride=PAIRS), :] = part[8 * g : 8 * g + 8]
+                    rows = atom_rows(GROUPS * (base + i) + j, g)
+                    flat[rows, :] = part[8 * g : 8 * g + 8]
+                    middle[rows, :] = sigma_t[rows, :] + part[8 * g : 8 * g + 8]
     copies = []
     for g in range(2):
         to_energy_rows(flat, sigma_here, g)
-        copies += send_half(sigma_here, sigma_ph, semaphores, g)
+        copies += move_half(sigma_here, sigma_ph, semaphores, g)
 
     for g in range(2):
-        def store(p, half, value):
-            flat_less[pl.ds(8 * g * PAIRS + p, 8, stride=PAIRS), :] = value
+        def store(p, value):
+            flat_less[atom_rows(p, g), :] = value
 
         sandwich_half(green_t, middle, g, store)
         to_energy_rows(flat_less, less_here, g)
-        copies += send_half(less_here, g_less, less_semaphores, g)
+        copies += move_half(less_here, g_less, less_semaphores, g)
     for copy in copies:
         copy.wait()
 
@@ -321,16 +325,16 @@
 
 
 def on_device(green, sigma_in, neighbours, coupling, send_down, send_up, offsets, w_emit, w_absorb):
-    whole = shape_of(PAIRS, NEAR, LANES, kind=F32)
+    tall = shape_of(NEAR * PITCH, LANES, kind=F32)
     half = shape_of(2 * EDGE, WIDTH)
     edge = shape_of(EDGE, WIDTH)
     given = (green, sigma_in, offsets, w_emit, w_absorb, neighbours.T, coupling.T, send_down, send_up)
     given = [pltpu.with_memory_space_constraint(array, pltpu.HBM) for array in given]
-    green_t, sigma_t, own, near, far, matrix, weights, pick, swapper = pl.pallas_call(
+    green_t, sigma_t, near, far, matrix, own_weights, edge_weights, pick, swapper = pl.pallas_call(
         lesser_kernel,
         out_shape=(
-            whole, whole, shape_of(ATOMS, WIDTH), half, half, shape_of(3 * LANES, LANES),
-            shape_of(ATOMS, 2 * (ATOMS + 2 * EDGE)), shape_of(2 * EDGE, 2 * EDGE), shape_of(WIDE, WIDE),
+            tall, tall, half, half, shape_of(3 * LANES, LANES), shape_of(ATOMS, 2 * ATOMS),
+            shape_of(ATOMS, 4 * EDGE), shape_of(2 * EDGE, 2 * EDGE), shape_of(WIDE, WIDE),
         ),
         in_specs=anywhere(9),
         out_specs=tuple(vmem(9)),
@@ -344,50 +348,52 @@
             pltpu.VMEM((1, EDGE), jnp.int32),
             pltpu.VMEM((ROWS, ATOMS * PAIRS), BF16),
             pltpu.VMEM((ROWS, ATOMS * PAIRS), BF16),
-            pltpu.VMEM((SPAN, LANES), F32),
             pltpu.VMEM((PAIRS, NEAR, LANES), F32),
             pltpu.VMEM((ATOMS, WIDTH), BF16),
+            pltpu.SemaphoreType.DMA((2 * GROUPS,)),
             pltpu.SemaphoreType.DMA((2 * GROUPS,)),
             pltpu.SemaphoreType.DMA((7,)),
         ],
         compiler_params=PARAMS,
     )(*given)
     near_apart = swap(near, "energy", 1)
+    near_beside = swap(near, "energy", 0)
     far_apart = swap(far, "energy", 1)
-    beside = swap(own, "energy", 0)
+    far_beside = swap(far, "energy", 0)
     near_done, first, second = pl.pallas_call(
         near_kernel,
         out_shape=(half, edge, edge),
         in_specs=vmem(5),
         out_specs=tuple(vmem(3)),
         compiler_params=PARAMS,
-    )(matrix, pick, near_apart, near, beside)
+    )(matrix, pick, near_apart, near, near_beside)
     first = swap(first, "slab", 0)
     second = swap(second, "slab", 1)
-    far_done = pl.pallas_call(
+    own = pl.pallas_call(
         far_kernel,
-        out_shape=half,
-        in_specs=vmem(4),
+        out_shape=shape_of(ATOMS, WIDTH, kind=F32),
+        in_specs=vmem(6),
         out_specs=vmem(1)[0],
+        scratch_shapes=[pltpu.VMEM((2 * EDGE, WIDTH), BF16)],
         compiler_params=PARAMS,
-    )(matrix, far_apart, far, beside)
+    )(matrix, own_weights, near_done, far_apart, far, far_beside)
     flat = shape_of(ROWS, ATOMS * PAIRS)
     return pl.pallas_call(
         final_kernel,
         out_shape=(flat, flat),
-        in_specs=vmem(8),
+        in_specs=vmem(7),
         out_specs=tuple(anywhere(2)),
         scratch_shapes=[
-            pltpu.VMEM((SPAN, LANES), F32),
-            pltpu.VMEM((SPAN, LANES), F32),
-            pltpu.VMEM((PAIRS, NEAR, LANES), F32),
+            pltpu.VMEM((NEAR * PITCH, LANES), F32),
+            pltpu.VMEM((NEAR * PITCH, LANES), F32),
+            pltpu.VMEM((NEAR * PITCH, LANES), F32),
             pltpu.VMEM((ROWS, ATOMS * PAIRS), BF16),
             pltpu.VMEM((ROWS, ATOMS * PAIRS), BF16),
             pltpu.SemaphoreType.DMA((2 * GROUPS,)),
             pltpu.SemaphoreType.DMA((2 * GROUPS,)),
         ],
         compiler_params=PARAMS,
-    )(weights, swapper, near_done, far_done, first, second, green_t, sigma_t)
+    )(edge_weights, swapper, own, first, second, green_t, sigma_t)
 
 
 def solution(mesh):

time: 32.7 us -> 30.4 us (0.930)
  Pallas kernels: 12.4 us -> 10.3 us
    pallas_call x3, Pallas kernels: 11.9 us -> 9.7 us  [the longest x1 4.99 us: on_device(): pl.pallas_call(lesser_kernel, out_shape=(tall, tall, half, half, shape_of...]
    ppermute x5 -> x6, waiting for transfers between devices: 7.18 us -> 6.9 us  [swap(): return lax.ppermute(block, axis, pairs)]
    ppermute x5 -> x6, starting transfers between devices: 12.3 us -> 12.3 us  [swap(): return lax.ppermute(block, axis, pairs)]
  transfers between devices with their start and end apart: 5 -> 6, of which waited for: 4 -> 4; matrix products, arithmetic and copies ran while one was open for 0% -> 0% of each run, Pallas kernels for 3% -> 4%
where the time goes in v2:
time: 30.4 us; the launch traced here: 30.2 us
  starting transfers between devices  12.3 us (40%)
  Pallas kernels  10.3 us (34%)
  waiting for transfers between devices  6.9 us (23%)
  between operations  0.7 us (2%)
    ppermute x6, starting transfers between devices, swap(): return lax.ppermute(block, axis, pairs)  12.3 us
    ppermute x6, waiting for transfers between devices, swap(): return lax.ppermute(block, axis, pairs)  6.9 us
    pallas_call x1, Pallas kernels, on_device(): pl.pallas_call(lesser_kernel, out_shape=(tall, tall, half, half, shape_of...  4.99 us
    pallas_call x1, Pallas kernels, on_device(): pl.pallas_call(final_kernel, out_shape=(flat, flat), in_specs=vmem(7), ou...  4.15 us
  transfers between devices with their start and end apart: 6, of which 4 were waited for; matrix products, arithmetic and copies ran while one was open for 0% of the time, Pallas kernels for 4%

profile of v2, /device:TPU:144, one launch (start us, length us, event | category | flops | bytes accessed | tf_op | source)
XLA Modules:
  0.0 30.2 jit_solution(14148630862716371052)
XLA Ops:
  0.6 5.0 %shard_map.104 = (f32[2320,128]{1,0:T(8,128)S(1)}, f32[2320,128]{1,0:T(8,128)S(1)}, bf16[32,4608]{1,0:T(8,128)(2,1)S(1)}, bf16[32,4608]{1,0:T(8,128)(2,1)S(1)}, ...) custom-call(bf16[32,9216]{1,0:T(8,128)(2,1)} %green.1, ...), custom_call_target="tpu_custom_call" | custom-call | tf_op jit(solution)/shard_map/pallas_call | solution.py:333
  5.6 0.1 collective-permute-start.1
  5.7 4.3 %collective-permute-start = (bf16[32,4608]{1,0:T(8,128)(2,1)S(1)}, bf16[32,4608]{1,0:T(8,128)(2,1)S(1)}, u32[]{:S(2)}, u32[]{:S(2)}) collective-permute-start(bf16[32,4608]{1,0:T(8,128)(2,1)S(1)} %get-tuple-element.19.here), channel_id=1, source_target_pairs={{4,8},{8,4},{12,16},{16,12},{20,24},{24,20},{28,32},{32,28},{36,40... | collective-permute-start | bytes 884744 | tf_op jit(solution)/shard_map/ppermute | solution.py:320
  10.0 0.1 collective-permute-start.3
  10.1 4.6 %collective-permute-start.2 = (bf16[32,4608]{1,0:T(8,128)(2,1)S(1)}, bf16[32,4608]{1,0:T(8,128)(2,1)S(1)}, u32[]{:S(2)}, u32[]{:S(2)}) collective-permute-start(bf16[32,4608]{1,0:T(8,128)(2,1)S(1)} %get-tuple-element.21.here), channel_id=1, source_target_pairs={{4,8},{8,4},{12,16},{16,12},{20,24},{24,20},{28,32},{32,28},{36,40... | collective-permute-start | bytes 884744 | tf_op jit(solution)/shard_map/ppermute | solution.py:320
  14.7 0.0 collective-permute-done.1.beside
  14.7 2.4 %collective-permute-done.apart = bf16[32,4608]{1,0:T(8,128)(2,1)S(1)} collective-permute-done((bf16[32,4608]{1,0:T(8,128)(2,1)S(1)}, bf16[32,4608]{1,0:T(8,128)(2,1)S(1)}, u32[]{:S(2)}, u32[]{:S(2)}) %collective-permute-start) | collective-permute-done | bytes 294944 | tf_op jit(solution)/shard_map/ppermute | solution.py:320
  17.1 0.6 %shard_map.105 = (bf16[32,4608]{1,0:T(8,128)(2,1)S(1)}, bf16[16,4608]{1,0:T(8,128)(2,1)S(1)}, bf16[16,4608]{1,0:T(8,128)(2,1)S(1)}) custom-call(bf16[384,128]{1,0:T(8,128)(2,1)S(1)} %get-tuple-element.16.matrix, bf16[32,32]{1,0:T(8,128)(2,1)S(1)} %get-tuple-element.18.pick, bf16[32,4608]{1,0:T(8,128)(2,1)S(1)} %collective-permute-done.apart, ...), custom_call_target="tpu_custom_call" | custom-call | tf_op jit(solution)/shard_map/pallas_call | solution.py:363
  17.7 1.4 %collective-permute-start.4 = (bf16[16,4608]{1,0:T(8,128)(2,1)S(1)}, bf16[16,4608]{1,0:T(8,128)(2,1)S(1)}, u32[]{:S(2)}, u32[]{:S(2)}) collective-permute-start(bf16[16,4608]{1,0:T(8,128)(2,1)S(1)} %get-tuple-element.22), channel_id=1, source_target_pairs={{0,1},{1,0},{2,3},{3,2},{4,5},{5,4},{6,7},{7,6},{8,9},{9,8},{10,11... | collective-permute-start | bytes 442376 | tf_op jit(solution)/shard_map/ppermute | solution.py:320
  19.0 1.9 %collective-permute-start.5 = (bf16[16,4608]{1,0:T(8,128)(2,1)S(1)}, bf16[16,4608]{1,0:T(8,128)(2,1)S(1)}, u32[]{:S(2)}, u32[]{:S(2)}) collective-permute-start(bf16[16,4608]{1,0:T(8,128)(2,1)S(1)} %get-tuple-element.23), channel_id=1, source_target_pairs={{1,2},{2,1},{5,6},{6,5},{9,10},{10,9},{13,14},{14,13},{17,18},{18,... | collective-permute-start | bytes 442376 | tf_op jit(solution)/shard_map/ppermute | solution.py:320
  20.9 0.0 collective-permute-done.3.beside
  21.0 0.5 %collective-permute-done.2.apart = bf16[32,4608]{1,0:T(8,128)(2,1)S(1)} collective-permute-done((bf16[32,4608]{1,0:T(8,128)(2,1)S(1)}, bf16[32,4608]{1,0:T(8,128)(2,1)S(1)}, u32[]{:S(2)}, u32[]{:S(2)}) %collective-permute-start.2) | collective-permute-done | bytes 294944 | tf_op jit(solution)/shard_map/ppermute | solution.py:320
  21.5 0.5 %shard_map.106.own = f32[64,4608]{1,0:T(8,128)S(1)} custom-call(bf16[384,128]{1,0:T(8,128)(2,1)S(1)} %get-tuple-element.16.matrix, bf16[64,128]{1,0:T(8,128)(2,1)S(1)} %get-tuple-element.17.weights, bf16[32,4608]{1,0:T(8,128)(2,1)S(1)} %get-tuple-element.20.near, bf16[32,4608]{1,0:T(8,128)(2,1)S(1)} %collective-permute-done.2.apart, ...), custom_call_target="tpu_custom_call" | custom-call | tf_op jit(solution)/shard_map/pallas_call | solution.py:372
  22.1 0.8 %collective-permute-done.4.first = bf16[16,4608]{1,0:T(8,128)(2,1)S(1)} collective-permute-done((bf16[16,4608]{1,0:T(8,128)(2,1)S(1)}, bf16[16,4608]{1,0:T(8,128)(2,1)S(1)}, u32[]{:S(2)}, u32[]{:S(2)}) %collective-permute-start.4) | collective-permute-done | bytes 147488 | tf_op jit(solution)/shard_map/ppermute | solution.py:320
  22.9 3.2 %collective-permute-done.5.second = bf16[16,4608]{1,0:T(8,128)(2,1)S(1)} collective-permute-done((bf16[16,4608]{1,0:T(8,128)(2,1)S(1)}, bf16[16,4608]{1,0:T(8,128)(2,1)S(1)}, u32[]{:S(2)}, u32[]{:S(2)}) %collective-permute-start.5) | collective-permute-done | bytes 147488 | tf_op jit(solution)/shard_map/ppermute | solution.py:320
  26.1 4.2 %shard_map.107 = (bf16[32,9216]{1,0:T(8,128)(2,1)}, bf16[32,9216]{1,0:T(8,128)(2,1)}) custom-call(bf16[64,64]{1,0:T(8,128)(2,1)S(1)} %get-tuple-element.14.weights, bf16[512,512]{1,0:T(8,128)(2,1)S(1)} %get-tuple-element.15.swapper, f32[64,4608]{1,0:T(8,128)S(1)} %shard_map.106.own, bf16[16,4608]{1,0:T(8,128)(2,1)S(1)} %collective-permute-done.4.first, ...), custom_call_target="tpu_custom_call" | custom-call | tf_op jit(solution)/shard_map/pallas_call | solution.py:381
Async XLA Ops:
  5.6 9.1 %collective-permute-start.1 = (bf16[32,4608]{1,0:T(8,128)(2,1)S(1)}, bf16[32,4608]{1,0:T(8,128)(2,1)S(1)}, u32[]{:S(2)}, u32[]{:S(2)}) collective-permute-start(bf16[32,4608]{1,0:T(8,128)(2,1)S(1)} %get-tuple-element.19.here), channel_id=1, source_target_pairs={{0,4},{4,0},{8,12},{12,8},{16,20},{20,16},{24,28},{28,24},{32,36},... | collective-permute-start | bytes 884744 | tf_op jit(solution)/shard_map/ppermute | solution.py:320
  5.7 11.4 %collective-permute-start = (bf16[32,4608]{1,0:T(8,128)(2,1)S(1)}, bf16[32,4608]{1,0:T(8,128)(2,1)S(1)}, u32[]{:S(2)}, u32[]{:S(2)}) collective-permute-start(bf16[32,4608]{1,0:T(8,128)(2,1)S(1)} %get-tuple-element.19.here), channel_id=1, source_target_pairs={{4,8},{8,4},{12,16},{16,12},{20,24},{24,20},{28,32},{32,28},{36,40... | collective-permute-start | bytes 884744 | tf_op jit(solution)/shard_map/ppermute | solution.py:320
  10.0 10.9 %collective-permute-start.3 = (bf16[32,4608]{1,0:T(8,128)(2,1)S(1)}, bf16[32,4608]{1,0:T(8,128)(2,1)S(1)}, u32[]{:S(2)}, u32[]{:S(2)}) collective-permute-start(bf16[32,4608]{1,0:T(8,128)(2,1)S(1)} %get-tuple-element.21.here), channel_id=1, source_target_pairs={{0,4},{4,0},{8,12},{12,8},{16,20},{20,16},{24,28},{28,24},{32,36},... | collective-permute-start | bytes 884744 | tf_op jit(solution)/shard_map/ppermute | solution.py:320
  10.1 11.4 %collective-permute-start.2 = (bf16[32,4608]{1,0:T(8,128)(2,1)S(1)}, bf16[32,4608]{1,0:T(8,128)(2,1)S(1)}, u32[]{:S(2)}, u32[]{:S(2)}) collective-permute-start(bf16[32,4608]{1,0:T(8,128)(2,1)S(1)} %get-tuple-element.21.here), channel_id=1, source_target_pairs={{4,8},{8,4},{12,16},{16,12},{20,24},{24,20},{28,32},{32,28},{36,40... | collective-permute-start | bytes 884744 | tf_op jit(solution)/shard_map/ppermute | solution.py:320
  17.7 5.2 %collective-permute-start.4 = (bf16[16,4608]{1,0:T(8,128)(2,1)S(1)}, bf16[16,4608]{1,0:T(8,128)(2,1)S(1)}, u32[]{:S(2)}, u32[]{:S(2)}) collective-permute-start(bf16[16,4608]{1,0:T(8,128)(2,1)S(1)} %get-tuple-element.22), channel_id=1, source_target_pairs={{0,1},{1,0},{2,3},{3,2},{4,5},{5,4},{6,7},{7,6},{8,9},{9,8},{10,11... | collective-permute-start | bytes 442376 | tf_op jit(solution)/shard_map/ppermute | solution.py:320
  19.0 7.0 %collective-permute-start.5 = (bf16[16,4608]{1,0:T(8,128)(2,1)S(1)}, bf16[16,4608]{1,0:T(8,128)(2,1)S(1)}, u32[]{:S(2)}, u32[]{:S(2)}) collective-permute-start(bf16[16,4608]{1,0:T(8,128)(2,1)S(1)} %get-tuple-element.23), channel_id=1, source_target_pairs={{1,2},{2,1},{5,6},{6,5},{9,10},{10,9},{13,14},{14,13},{17,18},{18,... | collective-permute-start | bytes 442376 | tf_op jit(solution)/shard_map/ppermute | solution.py:320

commit v3 on v2

--- a/solution.py
+++ b/solution.py
@@ -126,7 +126,7 @@
     return jnp.concatenate(rows, axis=0)
 
 
-def band(offsets, w_emit, w_absorb, odd):
+def band(offsets, w_emit, w_absorb, odd, end):
     shape = (ROWS, LANES)
     distance = lane_iota(shape) % ROWS - row_iota(shape)
     before = jnp.zeros(shape, F32)
@@ -137,7 +137,7 @@
         before = before + jnp.where(distance + ROWS == off, emit, 0.0)
         here = here + jnp.where(distance == off, emit, 0.0) + jnp.where(-distance == off, absorb, 0.0)
         after = after + jnp.where(ROWS - distance == off, absorb, 0.0)
-    apart = jnp.where(odd, after, before)
+    apart = jnp.where(end, 0.0, jnp.where(odd, after, before))
     beside = jnp.where(odd, before, after)
     group = lane_iota(shape) // ROWS
     parts = []
@@ -157,12 +157,13 @@
     return (row_iota(shape).astype(F32) == place).astype(BF16)
 
 
-def mixing(neighbours, coupling, order, odd):
+def mixing(neighbours, coupling, order, odd, lowest, highest):
     names = row_iota((ATOMS + 2 * EDGE, ATOMS))
     weights = jnp.zeros((ATOMS + 2 * EDGE, ATOMS), F32)
     for k in range(NBRS):
         weights = weights + jnp.where(names == neighbours[k : k + 1, :], coupling[k : k + 1, :], 0.0)
-    low, high = weights[ATOMS : ATOMS + EDGE], weights[ATOMS + EDGE :]
+    low = jnp.where(lowest, 0.0, weights[ATOMS : ATOMS + EDGE])
+    high = jnp.where(highest, 0.0, weights[ATOMS + EDGE :])
     edges = [jnp.where(odd, low, high), jnp.where(odd, high, low)]
     weights = jnp.concatenate([weights[:ATOMS]] + edges, axis=0)
     coarse = weights.astype(BF16)
@@ -191,17 +192,20 @@
     for copy in fetched:
         copy.wait()
     offsets, w_emit, w_absorb, neighbours, coupling, send_down, send_up = held
-    odd_slab = lax.axis_index("slab") % 2 == 1
-    odd_energy = lax.axis_index("energy") % 2 == 1
+    slab, energy = lax.axis_index("slab"), lax.axis_index("energy")
+    odd_energy = energy % 2 == 1
+    below = slab % 2 == 1
+    lowest, highest = slab == 0, slab == lax.axis_size("slab") - 1
+    end_energy = (energy == 0) | (energy == lax.axis_size("energy") - 1)
     down_hot = (row_iota((ATOMS, EDGE)) == send_down[...]).astype(F32)
     up_hot = (row_iota((ATOMS, EDGE)) == send_up[...]).astype(F32)
-    first_hot = jnp.where(odd_slab, down_hot, up_hot)
-    second_hot = jnp.where(odd_slab, up_hot, down_hot)
+    first_hot = jnp.where(below, down_hot, up_hot)
+    second_hot = jnp.where(below, up_hot, down_hot)
     order = atom_order(first_hot, second_hot)
     hot = jnp.concatenate([first_hot, second_hot], axis=1).astype(BF16)
     pick[...] = matmul(order[: 2 * EDGE], hot).astype(BF16)
-    own_weights[...], edge_weights[...] = mixing(neighbours, coupling, order, odd_slab)
-    matrix[...] = band(offsets, w_emit, w_absorb, odd_energy)
+    own_weights[...], edge_weights[...] = mixing(neighbours, coupling, order, below, lowest, highest)
+    matrix[...] = band(offsets, w_emit, w_absorb, odd_energy, end_energy)
     for n, (source, target) in enumerate(((green_here, green_t), (sigma_here, sigma_t))):
         for g in range(2):
             for copy in copies[2 * n + g]:
@@ -313,11 +317,39 @@
 PARAMS = pltpu.CompilerParams(vmem_limit_bytes=44 * 1024 * 1024)
 
 
-def swap(block, axis, parity):
+def pair_up(block, partner):
+    energies, slabs = lax.axis_size("energy"), lax.axis_size("slab")
     pairs = []
-    for i in range(parity, lax.axis_size(axis) - 1, 2):
-        pairs += [(i, i + 1), (i + 1, i)]
-    return lax.ppermute(block, axis, pairs)
+    for energy in range(energies):
+        for slab in range(slabs):
+            other_energy, other_slab = partner(energy, slab, energies, slabs)
+            pairs.append((energy * slabs + slab, other_energy * slabs + other_slab))
+    return lax.ppermute(block, ("energy", "slab"), pairs)
+
+
+def beside(energy, slab, energies, slabs):
+    return energy ^ 1, slab
+
+
+def apart(energy, slab, energies, slabs):
+    other = ((energy + 1) ^ 1) - 1
+    if 0 <= other < energies:
+        return other, slab
+    return energy, slab ^ 1
+
+
+def slab_step(energy, slab, slabs, step, aside):
+    if 0 <= slab + step < slabs:
+        return energy, slab + step
+    return energy ^ aside, slab
+
+
+def first_slab(energy, slab, energies, slabs):
+    return slab_step(energy, slab, slabs, 1 if slab % 2 == 0 else -1, 1)
+
+
+def second_slab(energy, slab, energies, slabs):
+    return slab_step(energy, slab, slabs, -1 if slab % 2 == 0 else 1, 1)
 
 
 def shape_of(*shape, kind=BF16):
@@ -356,10 +388,10 @@
         ],
         compiler_params=PARAMS,
     )(*given)
-    near_apart = swap(near, "energy", 1)
-    near_beside = swap(near, "energy", 0)
-    far_apart = swap(far, "energy", 1)
-    far_beside = swap(far, "energy", 0)
+    near_apart = pair_up(near, apart)
+    near_beside = pair_up(near, beside)
+    far_apart = pair_up(far, apart)
+    far_beside = pair_up(far, beside)
     near_done, first, second = pl.pallas_call(
         near_kernel,
         out_shape=(half, edge, edge),
@@ -367,8 +399,8 @@
         out_specs=tuple(vmem(3)),
         compiler_params=PARAMS,
     )(matrix, pick, near_apart, near, near_beside)
-    first = swap(first, "slab", 0)
-    second = swap(second, "slab", 1)
+    first = pair_up(first, first_slab)
+    second = pair_up(second, second_slab)
     own = pl.pallas_call(
         far_kernel,
         out_shape=shape_of(ATOMS, WIDTH, kind=F32),

time: 30.4 us -> 26.7 us (0.88)
  starting transfers between devices: 12.3 us -> 6.62 us
  waiting for transfers between devices: 6.9 us -> 8.99 us
    ppermute x6, starting transfers between devices: 12.3 us -> 6.62 us  [pair_up(): return lax.ppermute(block, ('energy', 'slab'), pairs)]
    ppermute x6, waiting for transfers between devices: 6.9 us -> 8.99 us  [pair_up(): return lax.ppermute(block, ('energy', 'slab'), pairs)]
where the time goes in v3:
time: 26.7 us; the launch traced here: 26.5 us
  Pallas kernels  10.3 us (39%)
  waiting for transfers between devices  8.99 us (34%)
  starting transfers between devices  6.62 us (25%)
  between operations  0.66 us (2%)
    ppermute x6, waiting for transfers between devices, pair_up(): return lax.ppermute(block, ('energy', 'slab'), pairs)  8.99 us
    ppermute x6, starting transfers between devices, pair_up(): return lax.ppermute(block, ('energy', 'slab'), pairs)  6.62 us
    pallas_call x1, Pallas kernels, on_device(): pl.pallas_call(lesser_kernel, out_shape=(tall, tall, half, half, shape_of...  4.99 us
    pallas_call x1, Pallas kernels, on_device(): pl.pallas_call(final_kernel, out_shape=(flat, flat), in_specs=vmem(7), ou...  4.16 us
    pallas_call x1, Pallas kernels, on_device(): pl.pallas_call(near_kernel, out_shape=(half, edge, edge), in_specs=vmem(5...  0.57 us
    pallas_call x1, Pallas kernels, on_device(): pl.pallas_call(far_kernel, out_shape=shape_of(ATOMS, WIDTH, kind=F32), in...  0.55 us
  transfers between devices with their start and end apart: 6, of which 4 were waited for; matrix products, arithmetic and copies ran while one was open for 0% of the time, Pallas kernels for 4%

profile of v3, /device:TPU:144, one launch (start us, length us, event | category | flops | bytes accessed | tf_op | source)
XLA Modules:
  0.0 26.5 jit_solution(7087221580700277019)
XLA Ops:
  0.6 5.0 %shard_map.104 = (f32[2320,128]{1,0:T(8,128)S(1)}, f32[2320,128]{1,0:T(8,128)S(1)}, bf16[32,4608]{1,0:T(8,128)(2,1)S(1)}, bf16[32,4608]{1,0:T(8,128)(2,1)S(1)}, ...) custom-call(bf16[32,9216]{1,0:T(8,128)(2,1)} %green.1, ...), custom_call_target="tpu_custom_call" | custom-call | tf_op jit(solution)/shard_map/pallas_call | solution.py:365
  5.6 0.1 collective-permute-start.1
  5.7 2.4 %collective-permute-start = (bf16[32,4608]{1,0:T(8,128)(2,1)S(1)}, bf16[32,4608]{1,0:T(8,128)(2,1)S(1)}, u32[]{:S(2)}, u32[]{:S(2)}) collective-permute-start(bf16[32,4608]{1,0:T(8,128)(2,1)S(1)} %get-tuple-element.19.here), channel_id=1, source_target_pairs={{0,1},{1,0},{2,3},{3,2},{4,8},{5,9},{6,10},{7,11},{8,4},{9,5},{10,... | collective-permute-start | bytes 884744 | tf_op jit(solution)/shard_map/ppermute | solution.py:327
  8.1 0.0 collective-permute-start.3
  8.1 2.7 %collective-permute-start.2 = (bf16[32,4608]{1,0:T(8,128)(2,1)S(1)}, bf16[32,4608]{1,0:T(8,128)(2,1)S(1)}, u32[]{:S(2)}, u32[]{:S(2)}) collective-permute-start(bf16[32,4608]{1,0:T(8,128)(2,1)S(1)} %get-tuple-element.21.here), channel_id=1, source_target_pairs={{0,1},{1,0},{2,3},{3,2},{4,8},{5,9},{6,10},{7,11},{8,4},{9,5},{10,... | collective-permute-start | bytes 884744 | tf_op jit(solution)/shard_map/ppermute | solution.py:327
  10.9 0.0 collective-permute-done.1.beside
  10.9 4.4 %collective-permute-done.apart = bf16[32,4608]{1,0:T(8,128)(2,1)S(1)} collective-permute-done((bf16[32,4608]{1,0:T(8,128)(2,1)S(1)}, bf16[32,4608]{1,0:T(8,128)(2,1)S(1)}, u32[]{:S(2)}, u32[]{:S(2)}) %collective-permute-start) | collective-permute-done | bytes 294944 | tf_op jit(solution)/shard_map/ppermute | solution.py:327
  15.3 0.6 %shard_map.105 = (bf16[32,4608]{1,0:T(8,128)(2,1)S(1)}, bf16[16,4608]{1,0:T(8,128)(2,1)S(1)}, bf16[16,4608]{1,0:T(8,128)(2,1)S(1)}) custom-call(bf16[384,128]{1,0:T(8,128)(2,1)S(1)} %get-tuple-element.16.matrix, bf16[32,32]{1,0:T(8,128)(2,1)S(1)} %get-tuple-element.18.pick, bf16[32,4608]{1,0:T(8,128)(2,1)S(1)} %collective-permute-done.apart, ...), custom_call_target="tpu_custom_call" | custom-call | tf_op jit(solution)/shard_map/pallas_call | solution.py:395
  15.9 1.4 %collective-permute-start.4 = (bf16[16,4608]{1,0:T(8,128)(2,1)S(1)}, bf16[16,4608]{1,0:T(8,128)(2,1)S(1)}, u32[]{:S(2)}, u32[]{:S(2)}) collective-permute-start(bf16[16,4608]{1,0:T(8,128)(2,1)S(1)} %get-tuple-element.22), channel_id=1, source_target_pairs={{0,1},{1,0},{2,3},{3,2},{4,5},{5,4},{6,7},{7,6},{8,9},{9,8},{10,11... | collective-permute-start | bytes 442376 | tf_op jit(solution)/shard_map/ppermute | solution.py:327
  17.2 0.0 collective-permute-start.5
  17.2 0.0 collective-permute-done.3.beside
  17.2 1.2 %collective-permute-done.2.apart = bf16[32,4608]{1,0:T(8,128)(2,1)S(1)} collective-permute-done((bf16[32,4608]{1,0:T(8,128)(2,1)S(1)}, bf16[32,4608]{1,0:T(8,128)(2,1)S(1)}, u32[]{:S(2)}, u32[]{:S(2)}) %collective-permute-start.2) | collective-permute-done | bytes 294944 | tf_op jit(solution)/shard_map/ppermute | solution.py:327
  18.4 0.5 %shard_map.106.own = f32[64,4608]{1,0:T(8,128)S(1)} custom-call(bf16[384,128]{1,0:T(8,128)(2,1)S(1)} %get-tuple-element.16.matrix, bf16[64,128]{1,0:T(8,128)(2,1)S(1)} %get-tuple-element.17.weights, bf16[32,4608]{1,0:T(8,128)(2,1)S(1)} %get-tuple-element.20.near, bf16[32,4608]{1,0:T(8,128)(2,1)S(1)} %collective-permute-done.2.apart, ...), custom_call_target="tpu_custom_call" | custom-call | tf_op jit(solution)/shard_map/pallas_call | solution.py:404
  19.0 2.1 %collective-permute-done.4.first = bf16[16,4608]{1,0:T(8,128)(2,1)S(1)} collective-permute-done((bf16[16,4608]{1,0:T(8,128)(2,1)S(1)}, bf16[16,4608]{1,0:T(8,128)(2,1)S(1)}, u32[]{:S(2)}, u32[]{:S(2)}) %collective-permute-start.4) | collective-permute-done | bytes 147488 | tf_op jit(solution)/shard_map/ppermute | solution.py:327
  21.1 1.3 %collective-permute-done.5.second = bf16[16,4608]{1,0:T(8,128)(2,1)S(1)} collective-permute-done((bf16[16,4608]{1,0:T(8,128)(2,1)S(1)}, bf16[16,4608]{1,0:T(8,128)(2,1)S(1)}, u32[]{:S(2)}, u32[]{:S(2)}) %collective-permute-start.5) | collective-permute-done | bytes 147488 | tf_op jit(solution)/shard_map/ppermute | solution.py:327
  22.4 4.2 %shard_map.107 = (bf16[32,9216]{1,0:T(8,128)(2,1)}, bf16[32,9216]{1,0:T(8,128)(2,1)}) custom-call(bf16[64,64]{1,0:T(8,128)(2,1)S(1)} %get-tuple-element.14.weights, bf16[512,512]{1,0:T(8,128)(2,1)S(1)} %get-tuple-element.15.swapper, f32[64,4608]{1,0:T(8,128)S(1)} %shard_map.106.own, bf16[16,4608]{1,0:T(8,128)(2,1)S(1)} %collective-permute-done.4.first, ...), custom_call_target="tpu_custom_call" | custom-call | tf_op jit(solution)/shard_map/pallas_call | solution.py:413
Async XLA Ops:
  5.6 5.3 %collective-permute-start.1 = (bf16[32,4608]{1,0:T(8,128)(2,1)S(1)}, bf16[32,4608]{1,0:T(8,128)(2,1)S(1)}, u32[]{:S(2)}, u32[]{:S(2)}) collective-permute-start(bf16[32,4608]{1,0:T(8,128)(2,1)S(1)} %get-tuple-element.19.here), channel_id=1, source_target_pairs={{0,4},{1,5},{2,6},{3,7},{4,0},{5,1},{6,2},{7,3},{8,12},{9,13},{10,... | collective-permute-start | bytes 884744 | tf_op jit(solution)/shard_map/ppermute | solution.py:327
  5.7 9.6 %collective-permute-start = (bf16[32,4608]{1,0:T(8,128)(2,1)S(1)}, bf16[32,4608]{1,0:T(8,128)(2,1)S(1)}, u32[]{:S(2)}, u32[]{:S(2)}) collective-permute-start(bf16[32,4608]{1,0:T(8,128)(2,1)S(1)} %get-tuple-element.19.here), channel_id=1, source_target_pairs={{0,1},{1,0},{2,3},{3,2},{4,8},{5,9},{6,10},{7,11},{8,4},{9,5},{10,... | collective-permute-start | bytes 884744 | tf_op jit(solution)/shard_map/ppermute | solution.py:327
  8.1 9.1 %collective-permute-start.3 = (bf16[32,4608]{1,0:T(8,128)(2,1)S(1)}, bf16[32,4608]{1,0:T(8,128)(2,1)S(1)}, u32[]{:S(2)}, u32[]{:S(2)}) collective-permute-start(bf16[32,4608]{1,0:T(8,128)(2,1)S(1)} %get-tuple-element.21.here), channel_id=1, source_target_pairs={{0,4},{1,5},{2,6},{3,7},{4,0},{5,1},{6,2},{7,3},{8,12},{9,13},{10,... | collective-permute-start | bytes 884744 | tf_op jit(solution)/shard_map/ppermute | solution.py:327
  8.1 10.3 %collective-permute-start.2 = (bf16[32,4608]{1,0:T(8,128)(2,1)S(1)}, bf16[32,4608]{1,0:T(8,128)(2,1)S(1)}, u32[]{:S(2)}, u32[]{:S(2)}) collective-permute-start(bf16[32,4608]{1,0:T(8,128)(2,1)S(1)} %get-tuple-element.21.here), channel_id=1, source_target_pairs={{0,1},{1,0},{2,3},{3,2},{4,8},{5,9},{6,10},{7,11},{8,4},{9,5},{10,... | collective-permute-start | bytes 884744 | tf_op jit(solution)/shard_map/ppermute | solution.py:327
  15.9 5.2 %collective-permute-start.4 = (bf16[16,4608]{1,0:T(8,128)(2,1)S(1)}, bf16[16,4608]{1,0:T(8,128)(2,1)S(1)}, u32[]{:S(2)}, u32[]{:S(2)}) collective-permute-start(bf16[16,4608]{1,0:T(8,128)(2,1)S(1)} %get-tuple-element.22), channel_id=1, source_target_pairs={{0,1},{1,0},{2,3},{3,2},{4,5},{5,4},{6,7},{7,6},{8,9},{9,8},{10,11... | collective-permute-start | bytes 442376 | tf_op jit(solution)/shard_map/ppermute | solution.py:327
  17.2 5.1 %collective-permute-start.5 = (bf16[16,4608]{1,0:T(8,128)(2,1)S(1)}, bf16[16,4608]{1,0:T(8,128)(2,1)S(1)}, u32[]{:S(2)}, u32[]{:S(2)}) collective-permute-start(bf16[16,4608]{1,0:T(8,128)(2,1)S(1)} %get-tuple-element.23), channel_id=1, source_target_pairs={{0,4},{1,2},{2,1},{3,7},{4,0},{5,6},{6,5},{7,3},{8,12},{9,10},{10,... | collective-permute-start | bytes 442376 | tf_op jit(solution)/shard_map/ppermute | solution.py:327

commit v4 on v3

--- a/solution.py
+++ b/solution.py
@@ -14,6 +14,8 @@
 ROWS = 32
 ATOMS = 64
 EDGE = 16
+REST = ATOMS - EDGE
+NAMED = ATOMS + EDGE
 NEAR = 16
 SPAN = NEAR * PAIRS
 PITCH = PAIRS + 1
@@ -147,14 +149,21 @@
 
 
 def atom_order(first_hot, second_hot):
-    edge = jnp.maximum(jnp.max(first_hot, axis=1, keepdims=True), jnp.max(second_hot, axis=1, keepdims=True))
+    in_first = jnp.max(first_hot, axis=1, keepdims=True)
+    edge = jnp.maximum(in_first, jnp.max(second_hot, axis=1, keepdims=True))
     shape = (ATOMS, ATOMS)
     earlier = jnp.sum(jnp.where(row_iota(shape) < lane_iota(shape), edge, 0.0), axis=0, keepdims=True)
-    itself = jnp.sum(jnp.where(row_iota(shape) == lane_iota(shape), edge, 0.0), axis=0, keepdims=True)
-    count = jnp.sum(jnp.broadcast_to(edge, shape), axis=0, keepdims=True)
-    number = lane_iota((1, ATOMS)).astype(F32)
-    place = jnp.where(itself > 0.5, earlier, count + number - earlier)
-    return (row_iota(shape).astype(F32) == place).astype(BF16)
+    itself = row_iota(shape) == lane_iota(shape)
+    in_edge = jnp.sum(jnp.where(itself, edge, 0.0), axis=0, keepdims=True)
+    in_first = jnp.sum(jnp.where(itself, in_first, 0.0), axis=0, keepdims=True)
+    place = jnp.where(in_edge > 0.5, -1.0, lane_iota((1, ATOMS)).astype(F32) - earlier)
+    rest = (row_iota((REST, ATOMS)).astype(F32) == place).astype(BF16)
+    eye = identity(EDGE)
+    first = flip(eye, first_hot.astype(BF16))
+    second = flip(eye, second_hot.astype(BF16))
+    order = jnp.concatenate([first.astype(BF16), second.astype(BF16), rest], axis=0)
+    once = jnp.concatenate([first.astype(BF16), (second * (1.0 - in_first)).astype(BF16), rest], axis=0)
+    return order, once
 
 
 def mixing(neighbours, coupling, order, odd, lowest, highest):
@@ -174,15 +183,12 @@
 
 
 def lesser_kernel(
-    green, sigma_in, *rest
+    green, sigma_in, down_list, up_list, green_t, sigma_t, near, far, once, swapper,
+    send_down, send_up, green_here, sigma_here, result, grouped, green_semaphores, sigma_semaphores, small_semaphores,
 ):
-    small = rest[:7]
-    green_t, sigma_t, near, far, matrix, own_weights, edge_weights, pick, swapper = rest[7:16]
-    held = rest[16:23]
-    green_here, sigma_here, result, grouped, green_semaphores, sigma_semaphores, small_semaphores = rest[23:]
     copies = []
     fetched = []
-    for n, (source, target) in enumerate(zip(small, held)):
+    for n, (source, target) in enumerate(((down_list, send_down), (up_list, send_up))):
         copy = pltpu.make_async_copy(source, target, small_semaphores.at[n])
         copy.start()
         fetched.append(copy)
@@ -191,21 +197,10 @@
     swapper[...] = chunk_swap()
     for copy in fetched:
         copy.wait()
-    offsets, w_emit, w_absorb, neighbours, coupling, send_down, send_up = held
-    slab, energy = lax.axis_index("slab"), lax.axis_index("energy")
-    odd_energy = energy % 2 == 1
-    below = slab % 2 == 1
-    lowest, highest = slab == 0, slab == lax.axis_size("slab") - 1
-    end_energy = (energy == 0) | (energy == lax.axis_size("energy") - 1)
+    below = lax.axis_index("slab") % 2 == 1
     down_hot = (row_iota((ATOMS, EDGE)) == send_down[...]).astype(F32)
     up_hot = (row_iota((ATOMS, EDGE)) == send_up[...]).astype(F32)
-    first_hot = jnp.where(below, down_hot, up_hot)
-    second_hot = jnp.where(below, up_hot, down_hot)
-    order = atom_order(first_hot, second_hot)
-    hot = jnp.concatenate([first_hot, second_hot], axis=1).astype(BF16)
-    pick[...] = matmul(order[: 2 * EDGE], hot).astype(BF16)
-    own_weights[...], edge_weights[...] = mixing(neighbours, coupling, order, below, lowest, highest)
-    matrix[...] = band(offsets, w_emit, w_absorb, odd_energy, end_energy)
+    order, once[...] = atom_order(jnp.where(below, down_hot, up_hot), jnp.where(below, up_hot, down_hot))
     for n, (source, target) in enumerate(((green_here, green_t), (sigma_here, sigma_t))):
         for g in range(2):
             for copy in copies[2 * n + g]:
@@ -235,33 +230,56 @@
         far[:, columns] = ordered[2 * EDGE :]
 
 
-def convolve(matrix, apart, here, beside, target):
+def stack(source, base):
+    return jnp.concatenate([source[:, q * LANES : (q + 1) * LANES] for q in range(base, base + BATCH)], axis=0)
+
+
+def here_kernel(
+    offset_list, emit_list, absorb_list, neighbour_list, coupling_list, once, near, near_beside,
+    matrix, own_weights, edge_weights, partial, offsets, w_emit, w_absorb, neighbours, coupling, semaphores,
+):
+    sources = (offset_list, emit_list, absorb_list, neighbour_list, coupling_list)
+    targets = (offsets, w_emit, w_absorb, neighbours, coupling)
+    copies = []
+    for n, (source, target) in enumerate(zip(sources, targets)):
+        copy = pltpu.make_async_copy(source, target, semaphores.at[n])
+        copy.start()
+        copies.append(copy)
+    for copy in copies:
+        copy.wait()
+    slab, energy = lax.axis_index("slab"), lax.axis_index("energy")
+    lowest, highest = slab == 0, slab == lax.axis_size("slab") - 1
+    end_energy = (energy == 0) | (energy == lax.axis_size("energy") - 1)
+    own_weights[...], edge_weights[...] = mixing(neighbours, coupling, once[...], slab % 2 == 1, lowest, highest)
+    matrix[...] = band(offsets, w_emit, w_absorb, energy % 2 == 1, end_energy)
     for base in range(0, QUADS, BATCH):
-        lhs = []
-        for source in (apart, here, beside):
-            lhs.append(jnp.concatenate(
-                [source[:, q * LANES : (q + 1) * LANES] for q in range(base, base + BATCH)], axis=0
-            ))
-        total = matmul(jnp.concatenate(lhs, axis=1), matrix[...]).astype(BF16)
+        lhs = jnp.concatenate([stack(near, base), stack(near_beside, base)], axis=1)
+        total = matmul(lhs, matrix[LANES:, :])
         for i in range(BATCH):
             column = (base + i) * LANES
-            target[:, column : column + LANES] = total[i * 2 * EDGE : (i + 1) * 2 * EDGE]
-
-
-def near_kernel(matrix, pick, apart, here, beside, target, first, second):
-    convolve(matrix, apart, here, beside, target)
+            partial[:, column : column + LANES] = total[i * 2 * EDGE : (i + 1) * 2 * EDGE]
+
+
+def near_kernel(matrix, near_apart, partial, first, second):
+    for base in range(0, QUADS, BATCH):
+        total = matmul(stack(near_apart, base), matrix[:LANES, :])
+        for i in range(BATCH):
+            columns = slice((base + i) * LANES, (base + i + 1) * LANES)
+            whole = (partial[:, columns] + total[i * 2 * EDGE : (i + 1) * 2 * EDGE]).astype(BF16)
+            first[:, columns] = whole[:EDGE]
+            second[:, columns] = whole[EDGE:]
+
+
+def far_kernel(matrix, weights, first, second, far_apart, far, far_beside, mixed, target):
+    for base in range(0, QUADS, BATCH):
+        lhs = jnp.concatenate([stack(source, base) for source in (far_apart, far, far_beside)], axis=1)
+        total = matmul(lhs, matrix[...]).astype(BF16)
+        for i in range(BATCH):
+            column = (base + i) * LANES
+            target[:, column : column + LANES] = total[i * REST : (i + 1) * REST]
     for t in range(WIDTH // WIDE):
         columns = slice(t * WIDE, (t + 1) * WIDE)
-        picked = matmul_first(pick[...], target[:, columns]).astype(BF16)
-        first[:, columns] = picked[:EDGE]
-        second[:, columns] = picked[EDGE:]
-
-
-def far_kernel(matrix, weights, near, apart, here, beside, mixed, target):
-    convolve(matrix, apart, here, beside, target)
-    for t in range(WIDTH // WIDE):
-        columns = slice(t * WIDE, (t + 1) * WIDE)
-        listed = [near[:, columns], target[:, columns]]
+        listed = [first[:, columns], second[:, columns], target[:, columns]]
         mixed[:, columns] = matmul(weights[...], jnp.concatenate(listed + listed, axis=0))
 
 
@@ -356,26 +374,20 @@
     return jax.ShapeDtypeStruct(shape, kind)
 
 
+def in_hbm(arrays):
+    return [pltpu.with_memory_space_constraint(array, pltpu.HBM) for array in arrays]
+
+
 def on_device(green, sigma_in, neighbours, coupling, send_down, send_up, offsets, w_emit, w_absorb):
     tall = shape_of(NEAR * PITCH, LANES, kind=F32)
     half = shape_of(2 * EDGE, WIDTH)
     edge = shape_of(EDGE, WIDTH)
-    given = (green, sigma_in, offsets, w_emit, w_absorb, neighbours.T, coupling.T, send_down, send_up)
-    given = [pltpu.with_memory_space_constraint(array, pltpu.HBM) for array in given]
-    green_t, sigma_t, near, far, matrix, own_weights, edge_weights, pick, swapper = pl.pallas_call(
+    green_t, sigma_t, near, far, once, swapper = pl.pallas_call(
         lesser_kernel,
-        out_shape=(
-            tall, tall, half, half, shape_of(3 * LANES, LANES), shape_of(ATOMS, 2 * ATOMS),
-            shape_of(ATOMS, 4 * EDGE), shape_of(2 * EDGE, 2 * EDGE), shape_of(WIDE, WIDE),
-        ),
-        in_specs=anywhere(9),
-        out_specs=tuple(vmem(9)),
+        out_shape=(tall, tall, half, shape_of(REST, WIDTH), shape_of(NAMED, ATOMS), shape_of(WIDE, WIDE)),
+        in_specs=anywhere(4),
+        out_specs=tuple(vmem(6)),
         scratch_shapes=[
-            pltpu.SMEM((FREQS,), jnp.int32),
-            pltpu.SMEM((FREQS,), F32),
-            pltpu.SMEM((FREQS,), F32),
-            pltpu.VMEM((NBRS, ATOMS), jnp.int32),
-            pltpu.VMEM((NBRS, ATOMS), F32),
             pltpu.VMEM((1, EDGE), jnp.int32),
             pltpu.VMEM((1, EDGE), jnp.int32),
             pltpu.VMEM((ROWS, ATOMS * PAIRS), BF16),
@@ -384,31 +396,49 @@
             pltpu.VMEM((ATOMS, WIDTH), BF16),
             pltpu.SemaphoreType.DMA((2 * GROUPS,)),
             pltpu.SemaphoreType.DMA((2 * GROUPS,)),
-            pltpu.SemaphoreType.DMA((7,)),
+            pltpu.SemaphoreType.DMA((2,)),
         ],
         compiler_params=PARAMS,
-    )(*given)
+    )(*in_hbm((green, sigma_in, send_down, send_up)))
     near_apart = pair_up(near, apart)
     near_beside = pair_up(near, beside)
     far_apart = pair_up(far, apart)
     far_beside = pair_up(far, beside)
-    near_done, first, second = pl.pallas_call(
+    matrix, own_weights, edge_weights, partial = pl.pallas_call(
+        here_kernel,
+        out_shape=(
+            shape_of(3 * LANES, LANES), shape_of(ATOMS, 2 * NAMED), shape_of(ATOMS, 4 * EDGE),
+            shape_of(2 * EDGE, WIDTH, kind=F32),
+        ),
+        in_specs=anywhere(5) + vmem(3),
+        out_specs=tuple(vmem(4)),
+        scratch_shapes=[
+            pltpu.SMEM((FREQS,), jnp.int32),
+            pltpu.SMEM((FREQS,), F32),
+            pltpu.SMEM((FREQS,), F32),
+            pltpu.VMEM((NBRS, ATOMS), jnp.int32),
+            pltpu.VMEM((NBRS, ATOMS), F32),
+            pltpu.SemaphoreType.DMA((5,)),
+        ],
+        compiler_params=PARAMS,
+    )(*in_hbm((offsets, w_emit, w_absorb, neighbours.T, coupling.T)), once, near, near_beside)
+    first, second = pl.pallas_call(
         near_kernel,
-        out_shape=(half, edge, edge),
-        in_specs=vmem(5),
-        out_specs=tuple(vmem(3)),
+        out_shape=(edge, edge),
+        in_specs=vmem(3),
+        out_specs=tuple(vmem(2)),
         compiler_params=PARAMS,
-    )(matrix, pick, near_apart, near, near_beside)
-    first = pair_up(first, first_slab)
-    second = pair_up(second, second_slab)
+    )(matrix, near_apart, partial)
     own = pl.pallas_call(
         far_kernel,
         out_shape=shape_of(ATOMS, WIDTH, kind=F32),
-        in_specs=vmem(6),
+        in_specs=vmem(7),
         out_specs=vmem(1)[0],
-        scratch_shapes=[pltpu.VMEM((2 * EDGE, WIDTH), BF16)],
+        scratch_shapes=[pltpu.VMEM((REST, WIDTH), BF16)],
         compiler_params=PARAMS,
-    )(matrix, own_weights, near_done, far_apart, far, far_beside)
+    )(matrix, own_weights, first, second, far_apart, far, far_beside)
+    first = pair_up(first, first_slab)
+    second = pair_up(second, second_slab)
     flat = shape_of(ROWS, ATOMS * PAIRS)
     return pl.pallas_call(
         final_kernel,

time: 26.7 us -> 25.9 us (0.970)
  waiting for transfers between devices: 8.99 us -> 7.58 us
  Pallas kernels: 10.3 us -> 10.9 us
    ppermute x6, waiting for transfers between devices: 8.99 us -> 7.58 us  [pair_up(): return lax.ppermute(block, ('energy', 'slab'), pairs)]
    pallas_call x2 -> x3, Pallas kernels: 5.55 us -> 6.07 us  [the longest x1 4.59 us: on_device(): pl.pallas_call(lesser_kernel, out_shape=(tall, tall, half, shape_of(REST,...]
  transfers between devices with their start and end apart: 6 -> 6, of which waited for: 4 -> 3; matrix products, arithmetic and copies ran while one was open for 0% -> 0% of each run, Pallas kernels for 4% -> 8%
where the time goes in v4:
time: 25.9 us; the launch traced here: 25.8 us
  Pallas kernels  10.9 us (42%)
  waiting for transfers between devices  7.58 us (29%)
  starting transfers between devices  6.62 us (26%)
  between operations  0.67 us (3%)
    ppermute x6, waiting for transfers between devices, pair_up(): return lax.ppermute(block, ('energy', 'slab'), pairs)  7.58 us
    ppermute x6, starting transfers between devices, pair_up(): return lax.ppermute(block, ('energy', 'slab'), pairs)  6.62 us
    pallas_call x1, Pallas kernels, on_device(): pl.pallas_call(lesser_kernel, out_shape=(tall, tall, half, shape_of(REST,...  4.59 us
    pallas_call x1, Pallas kernels, on_device(): pl.pallas_call(final_kernel, out_shape=(flat, flat), in_specs=vmem(7), ou...  4.15 us
    pallas_call x1, Pallas kernels, on_device(): pl.pallas_call(here_kernel, out_shape=(shape_of(3 * LANES, LANES), shape_...  1.26 us
    pallas_call x1, Pallas kernels, on_device(): pl.pallas_call(far_kernel, out_shape=shape_of(ATOMS, WIDTH, kind=F32), in...  0.69 us
  transfers between devices with their start and end apart: 6, of which 3 were waited for; matrix products, arithmetic and copies ran while one was open for 0% of the time, Pallas kernels for 8%

profile of v4, /device:TPU:144, one launch (start us, length us, event | category | flops | bytes accessed | tf_op | source)
XLA Modules:
  0.0 25.8 jit_solution(8541041482523491004)
XLA Ops:
  0.6 4.6 %shard_map.104 = (f32[2320,128]{1,0:T(8,128)S(1)}, f32[2320,128]{1,0:T(8,128)S(1)}, bf16[32,4608]{1,0:T(8,128)(2,1)S(1)}, bf16[48,4608]{1,0:T(8,128)(2,1)S(1)}, ...) custom-call(bf16[32,9216]{1,0:T(8,128)(2,1)} %green.1, bf16[32,9216]{1,0:T(8,128)(2,1)} %sigma_in.1, ...), custom_call_target="tpu_custom_call" | custom-call | tf_op jit(solution)/shard_map/pallas_call | solution.py:385
  5.2 0.1 collective-permute-start
  5.3 2.4 %collective-permute-start.1 = (bf16[32,4608]{1,0:T(8,128)(2,1)S(1)}, bf16[32,4608]{1,0:T(8,128)(2,1)S(1)}, u32[]{:S(2)}, u32[]{:S(2)}) collective-permute-start(bf16[32,4608]{1,0:T(8,128)(2,1)S(1)} %get-tuple-element.15.near), channel_id=1, source_target_pairs={{0,1},{1,0},{2,3},{3,2},{4,8},{5,9},{6,10},{7,11},{8,4},{9,5},{10,... | collective-permute-start | bytes 884744 | tf_op jit(solution)/shard_map/ppermute | solution.py:345
  7.7 2.7 %collective-permute-start.2 = (bf16[48,4608]{1,0:T(8,128)(2,1)S(1)}, bf16[48,4608]{1,0:T(8,128)(2,1)S(1)}, u32[]{:S(2)}, u32[]{:S(2)}) collective-permute-start(bf16[48,4608]{1,0:T(8,128)(2,1)S(1)} %get-tuple-element.23.far), channel_id=1, source_target_pairs={{0,1},{1,0},{2,3},{3,2},{4,8},{5,9},{6,10},{7,11},{8,4},{9,5},{10,... | collective-permute-start | bytes 1327112 | tf_op jit(solution)/shard_map/ppermute | solution.py:345
  10.5 0.0 collective-permute-start.3
  10.5 0.0 collective-permute-done.near_beside
  10.5 1.3 %shard_map.105 = (bf16[384,128]{1,0:T(8,128)(2,1)S(1)}, bf16[64,160]{1,0:T(8,128)(2,1)S(1)}, bf16[64,64]{1,0:T(8,128)(2,1)S(1)}, f32[32,4608]{1,0:T(8,128)S(1)}) custom-call(s32[16]{0:T(128)} %offset_list.1, f32[16]{0:T(128)} %emit_list.1, f32[16]{0:T(128)} %absorb_list.1, s32[8,64]{1,0:T(8,128)} %bitcast.2, f32[8,64]{1,0:T(8,128)} %bitcast.3, ...), custom_call_target="tpu_custom_call" | custom-call | tf_op jit(solution)/shard_map/pallas_call | solution.py:407
  11.8 3.1 %collective-permute-done.1.near_apart = bf16[32,4608]{1,0:T(8,128)(2,1)S(1)} collective-permute-done((bf16[32,4608]{1,0:T(8,128)(2,1)S(1)}, bf16[32,4608]{1,0:T(8,128)(2,1)S(1)}, u32[]{:S(2)}, u32[]{:S(2)}) %collective-permute-start.1) | collective-permute-done | bytes 294944 | tf_op jit(solution)/shard_map/ppermute | solution.py:345
  14.9 0.2 shard_map.106
  15.1 1.4 %collective-permute-start.4 = (bf16[16,4608]{1,0:T(8,128)(2,1)S(1)}, bf16[16,4608]{1,0:T(8,128)(2,1)S(1)}, u32[]{:S(2)}, u32[]{:S(2)}) collective-permute-start(bf16[16,4608]{1,0:T(8,128)(2,1)S(1)} %get-tuple-element.21.first), channel_id=1, source_target_pairs={{0,1},{1,0},{2,3},{3,2},{4,5},{5,4},{6,7},{7,6},{8,9},{9,8},{10,11... | collective-permute-start | bytes 442376 | tf_op jit(solution)/shard_map/ppermute | solution.py:345
  16.5 0.0 collective-permute-start.5
  16.5 3.1 %collective-permute-done.2.far_apart = bf16[48,4608]{1,0:T(8,128)(2,1)S(1)} collective-permute-done((bf16[48,4608]{1,0:T(8,128)(2,1)S(1)}, bf16[48,4608]{1,0:T(8,128)(2,1)S(1)}, u32[]{:S(2)}, u32[]{:S(2)}) %collective-permute-start.2) | collective-permute-done | bytes 442400 | tf_op jit(solution)/shard_map/ppermute | solution.py:345
  19.6 0.0 collective-permute-done.3.far_beside
  19.6 0.7 %shard_map.107.own = f32[64,4608]{1,0:T(8,128)S(1)} custom-call(bf16[384,128]{1,0:T(8,128)(2,1)S(1)} %get-tuple-element.18.matrix, bf16[64,160]{1,0:T(8,128)(2,1)S(1)} %get-tuple-element.19.weights, bf16[16,4608]{1,0:T(8,128)(2,1)S(1)} %get-tuple-element.21.first, bf16[16,4608]{1,0:T(8,128)(2,1)S(1)} %get-tuple-element.22.second, ...), custom_call_target="tpu_custom_call" | custom-call | tf_op jit(solution)/shard_map/pallas_call | solution.py:432
  20.3 0.0 collective-permute-done.4.first
  20.3 1.3 %collective-permute-done.5.second = bf16[16,4608]{1,0:T(8,128)(2,1)S(1)} collective-permute-done((bf16[16,4608]{1,0:T(8,128)(2,1)S(1)}, bf16[16,4608]{1,0:T(8,128)(2,1)S(1)}, u32[]{:S(2)}, u32[]{:S(2)}) %collective-permute-start.5) | collective-permute-done | bytes 147488 | tf_op jit(solution)/shard_map/ppermute | solution.py:345
  21.6 4.2 %shard_map.108 = (bf16[32,9216]{1,0:T(8,128)(2,1)}, bf16[32,9216]{1,0:T(8,128)(2,1)}) custom-call(bf16[64,64]{1,0:T(8,128)(2,1)S(1)} %get-tuple-element.16.weights, bf16[512,512]{1,0:T(8,128)(2,1)S(1)} %get-tuple-element.17.swapper, f32[64,4608]{1,0:T(8,128)S(1)} %shard_map.107.own, bf16[16,4608]{1,0:T(8,128)(2,1)S(1)} %collective-permute-done.4.first, ...), custom_call_target="tpu_custom_call" | custom-call | tf_op jit(solution)/shard_map/pallas_call | solution.py:443
Async XLA Ops:
  5.2 5.3 %collective-permute-start = (bf16[32,4608]{1,0:T(8,128)(2,1)S(1)}, bf16[32,4608]{1,0:T(8,128)(2,1)S(1)}, u32[]{:S(2)}, u32[]{:S(2)}) collective-permute-start(bf16[32,4608]{1,0:T(8,128)(2,1)S(1)} %get-tuple-element.15.near), channel_id=1, source_target_pairs={{0,4},{1,5},{2,6},{3,7},{4,0},{5,1},{6,2},{7,3},{8,12},{9,13},{10,... | collective-permute-start | bytes 884744 | tf_op jit(solution)/shard_map/ppermute | solution.py:345
  5.3 9.6 %collective-permute-start.1 = (bf16[32,4608]{1,0:T(8,128)(2,1)S(1)}, bf16[32,4608]{1,0:T(8,128)(2,1)S(1)}, u32[]{:S(2)}, u32[]{:S(2)}) collective-permute-start(bf16[32,4608]{1,0:T(8,128)(2,1)S(1)} %get-tuple-element.15.near), channel_id=1, source_target_pairs={{0,1},{1,0},{2,3},{3,2},{4,8},{5,9},{6,10},{7,11},{8,4},{9,5},{10,... | collective-permute-start | bytes 884744 | tf_op jit(solution)/shard_map/ppermute | solution.py:345
  7.7 11.9 %collective-permute-start.2 = (bf16[48,4608]{1,0:T(8,128)(2,1)S(1)}, bf16[48,4608]{1,0:T(8,128)(2,1)S(1)}, u32[]{:S(2)}, u32[]{:S(2)}) collective-permute-start(bf16[48,4608]{1,0:T(8,128)(2,1)S(1)} %get-tuple-element.23.far), channel_id=1, source_target_pairs={{0,1},{1,0},{2,3},{3,2},{4,8},{5,9},{6,10},{7,11},{8,4},{9,5},{10,... | collective-permute-start | bytes 1327112 | tf_op jit(solution)/shard_map/ppermute | solution.py:345
  10.5 9.1 %collective-permute-start.3 = (bf16[48,4608]{1,0:T(8,128)(2,1)S(1)}, bf16[48,4608]{1,0:T(8,128)(2,1)S(1)}, u32[]{:S(2)}, u32[]{:S(2)}) collective-permute-start(bf16[48,4608]{1,0:T(8,128)(2,1)S(1)} %get-tuple-element.23.far), channel_id=1, source_target_pairs={{0,4},{1,5},{2,6},{3,7},{4,0},{5,1},{6,2},{7,3},{8,12},{9,13},{10,... | collective-permute-start | bytes 1327112 | tf_op jit(solution)/shard_map/ppermute | solution.py:345
  15.1 5.2 %collective-permute-start.4 = (bf16[16,4608]{1,0:T(8,128)(2,1)S(1)}, bf16[16,4608]{1,0:T(8,128)(2,1)S(1)}, u32[]{:S(2)}, u32[]{:S(2)}) collective-permute-start(bf16[16,4608]{1,0:T(8,128)(2,1)S(1)} %get-tuple-element.21.first), channel_id=1, source_target_pairs={{0,1},{1,0},{2,3},{3,2},{4,5},{5,4},{6,7},{7,6},{8,9},{9,8},{10,11... | collective-permute-start | bytes 442376 | tf_op jit(solution)/shard_map/ppermute | solution.py:345
  16.5 5.1 %collective-permute-start.5 = (bf16[16,4608]{1,0:T(8,128)(2,1)S(1)}, bf16[16,4608]{1,0:T(8,128)(2,1)S(1)}, u32[]{:S(2)}, u32[]{:S(2)}) collective-permute-start(bf16[16,4608]{1,0:T(8,128)(2,1)S(1)} %get-tuple-element.22.second), channel_id=1, source_target_pairs={{0,4},{1,2},{2,1},{3,7},{4,0},{5,6},{6,5},{7,3},{8,12},{9,10},{10,... | collective-permute-start | bytes 442376 | tf_op jit(solution)/shard_map/ppermute | solution.py:345

commit v5 on v4

--- a/solution.py
+++ b/solution.py
@@ -24,6 +24,7 @@
 WIDTH = PAIRS * ROWS
 WIDE = 512
 BATCH = 12
+LAST = 36
 F32 = jnp.float32
 BF16 = jnp.bfloat16
 
@@ -192,8 +193,9 @@
         copy = pltpu.make_async_copy(source, target, small_semaphores.at[n])
         copy.start()
         fetched.append(copy)
-    for source, target, semaphores in ((green, green_here, green_semaphores), (sigma_in, sigma_here, sigma_semaphores)):
-        copies += [move_half(source, target, semaphores, g) for g in range(2)]
+    moves = ((green, green_here, green_semaphores), (sigma_in, sigma_here, sigma_semaphores))
+    for g in range(2):
+        copies.append([move_half(source, target, semaphores, g) for source, target, semaphores in moves])
     swapper[...] = chunk_swap()
     for copy in fetched:
         copy.wait()
@@ -201,12 +203,12 @@
     down_hot = (row_iota((ATOMS, EDGE)) == send_down[...]).astype(F32)
     up_hot = (row_iota((ATOMS, EDGE)) == send_up[...]).astype(F32)
     order, once[...] = atom_order(jnp.where(below, down_hot, up_hot), jnp.where(below, up_hot, down_hot))
-    for n, (source, target) in enumerate(((green_here, green_t), (sigma_here, sigma_t))):
-        for g in range(2):
-            for copy in copies[2 * n + g]:
+    for g in range(2):
+        for started, source, target in zip(copies[g], (green_here, sigma_here), (green_t, sigma_t)):
+            for copy in started:
                 copy.wait()
             to_batch_lanes(source, target, g)
-    for g in range(2):
+
         def store(p, value):
             result[p, 8 * g : 8 * g + 8, :] = value
 
@@ -287,9 +289,9 @@
     weights, swapper, own, first, second, green_t, sigma_t, sigma_ph, g_less,
     flat, flat_less, middle, sigma_here, less_here, semaphores, less_semaphores,
 ):
-    for base in range(0, QUADS, BATCH):
+    for base in range(0, QUADS, LAST):
         parts = []
-        for t in range(base * LANES // WIDE, (base + BATCH) * LANES // WIDE):
+        for t in range(base * LANES // WIDE, (base + LAST) * LANES // WIDE):
             columns = slice(t * WIDE, (t + 1) * WIDE)
             listed = [first[:, columns], second[:, columns]]
             edges = matmul(weights[...], jnp.concatenate(listed + listed, axis=0))
@@ -298,10 +300,10 @@
         columns = []
         for h in range(GROUPS):
             columns.append(jnp.concatenate(
-                [mixed[h * NEAR : (h + 1) * NEAR, i * LANES : (i + 1) * LANES] for i in range(BATCH)], axis=0
+                [mixed[h * NEAR : (h + 1) * NEAR, i * LANES : (i + 1) * LANES] for i in range(LAST)], axis=0
             ))
         moved = matmul(jnp.concatenate(columns, axis=1), swapper[...])
-        for i in range(BATCH):
+        for i in range(LAST):
             for j in range(GROUPS):
                 part = moved[i * NEAR : (i + 1) * NEAR, j * LANES : (j + 1) * LANES]
                 for g in range(2):
@@ -309,9 +311,8 @@
                     flat[rows, :] = part[8 * g : 8 * g + 8]
                     middle[rows, :] = sigma_t[rows, :] + part[8 * g : 8 * g + 8]
     copies = []
-    for g in range(2):
-        to_energy_rows(flat, sigma_here, g)
-        copies += move_half(sigma_here, sigma_ph, semaphores, g)
+    to_energy_rows(flat, sigma_here, 0)
+    copies += move_half(sigma_here, sigma_ph, semaphores, 0)
 
     for g in range(2):
         def store(p, value):
@@ -320,6 +321,9 @@
         sandwich_half(green_t, middle, g, store)
         to_energy_rows(flat_less, less_here, g)
         copies += move_half(less_here, g_less, less_semaphores, g)
+        if g == 0:
+            to_energy_rows(flat, sigma_here, 1)
+            copies += move_half(sigma_here, sigma_ph, semaphores, 1)
     for copy in copies:
         copy.wait()
 

time: 25.9 us -> 25.7 us (level)
  no operation moved by 1% of the time
where the time goes in v5:
time: 25.7 us; the launch traced here: 25.5 us
  Pallas kernels  10.7 us (42%)
  waiting for transfers between devices  7.58 us (29%)
  starting transfers between devices  6.62 us (26%)
  between operations  0.67 us (3%)
    ppermute x6, waiting for transfers between devices, pair_up(): return lax.ppermute(block, ('energy', 'slab'), pairs)  7.58 us
    ppermute x6, starting transfers between devices, pair_up(): return lax.ppermute(block, ('energy', 'slab'), pairs)  6.62 us
    pallas_call x1, Pallas kernels, on_device(): pl.pallas_call(lesser_kernel, out_shape=(tall, tall, half, shape_of(REST,...  4.59 us
    pallas_call x1, Pallas kernels, on_device(): pl.pallas_call(final_kernel, out_shape=(flat, flat), in_specs=vmem(7), ou...  3.91 us
    pallas_call x1, Pallas kernels, on_device(): pl.pallas_call(here_kernel, out_shape=(shape_of(3 * LANES, LANES), shape_...  1.26 us
    pallas_call x1, Pallas kernels, on_device(): pl.pallas_call(far_kernel, out_shape=shape_of(ATOMS, WIDTH, kind=F32), in...  0.69 us
  transfers between devices with their start and end apart: 6, of which 3 were waited for; matrix products, arithmetic and copies ran while one was open for 0% of the time, Pallas kernels for 8%

profile of v5, /device:TPU:144, one launch (start us, length us, event | category | flops | bytes accessed | tf_op | source)
XLA Modules:
  0.0 25.5 jit_solution(3618628554541487854)
XLA Ops:
  0.6 4.6 %shard_map.104 = (f32[2320,128]{1,0:T(8,128)S(1)}, f32[2320,128]{1,0:T(8,128)S(1)}, bf16[32,4608]{1,0:T(8,128)(2,1)S(1)}, bf16[48,4608]{1,0:T(8,128)(2,1)S(1)}, ...) custom-call(bf16[32,9216]{1,0:T(8,128)(2,1)} %green.1, bf16[32,9216]{1,0:T(8,128)(2,1)} %sigma_in.1, ...), custom_call_target="tpu_custom_call" | custom-call | tf_op jit(solution)/shard_map/pallas_call | solution.py:389
  5.2 0.1 collective-permute-start
  5.3 2.4 %collective-permute-start.1 = (bf16[32,4608]{1,0:T(8,128)(2,1)S(1)}, bf16[32,4608]{1,0:T(8,128)(2,1)S(1)}, u32[]{:S(2)}, u32[]{:S(2)}) collective-permute-start(bf16[32,4608]{1,0:T(8,128)(2,1)S(1)} %get-tuple-element.15.near), channel_id=1, source_target_pairs={{0,1},{1,0},{2,3},{3,2},{4,8},{5,9},{6,10},{7,11},{8,4},{9,5},{10,... | collective-permute-start | bytes 884744 | tf_op jit(solution)/shard_map/ppermute | solution.py:349
  7.7 2.7 %collective-permute-start.2 = (bf16[48,4608]{1,0:T(8,128)(2,1)S(1)}, bf16[48,4608]{1,0:T(8,128)(2,1)S(1)}, u32[]{:S(2)}, u32[]{:S(2)}) collective-permute-start(bf16[48,4608]{1,0:T(8,128)(2,1)S(1)} %get-tuple-element.23.far), channel_id=1, source_target_pairs={{0,1},{1,0},{2,3},{3,2},{4,8},{5,9},{6,10},{7,11},{8,4},{9,5},{10,... | collective-permute-start | bytes 1327112 | tf_op jit(solution)/shard_map/ppermute | solution.py:349
  10.5 0.0 collective-permute-start.3
  10.5 0.0 collective-permute-done.near_beside
  10.5 1.3 %shard_map.105 = (bf16[384,128]{1,0:T(8,128)(2,1)S(1)}, bf16[64,160]{1,0:T(8,128)(2,1)S(1)}, bf16[64,64]{1,0:T(8,128)(2,1)S(1)}, f32[32,4608]{1,0:T(8,128)S(1)}) custom-call(s32[16]{0:T(128)} %offset_list.1, f32[16]{0:T(128)} %emit_list.1, f32[16]{0:T(128)} %absorb_list.1, s32[8,64]{1,0:T(8,128)} %bitcast.2, f32[8,64]{1,0:T(8,128)} %bitcast.3, ...), custom_call_target="tpu_custom_call" | custom-call | tf_op jit(solution)/shard_map/pallas_call | solution.py:411
  11.8 3.1 %collective-permute-done.1.near_apart = bf16[32,4608]{1,0:T(8,128)(2,1)S(1)} collective-permute-done((bf16[32,4608]{1,0:T(8,128)(2,1)S(1)}, bf16[32,4608]{1,0:T(8,128)(2,1)S(1)}, u32[]{:S(2)}, u32[]{:S(2)}) %collective-permute-start.1) | collective-permute-done | bytes 294944 | tf_op jit(solution)/shard_map/ppermute | solution.py:349
  14.9 0.2 shard_map.106
  15.1 1.4 %collective-permute-start.4 = (bf16[16,4608]{1,0:T(8,128)(2,1)S(1)}, bf16[16,4608]{1,0:T(8,128)(2,1)S(1)}, u32[]{:S(2)}, u32[]{:S(2)}) collective-permute-start(bf16[16,4608]{1,0:T(8,128)(2,1)S(1)} %get-tuple-element.21.first), channel_id=1, source_target_pairs={{0,1},{1,0},{2,3},{3,2},{4,5},{5,4},{6,7},{7,6},{8,9},{9,8},{10,11... | collective-permute-start | bytes 442376 | tf_op jit(solution)/shard_map/ppermute | solution.py:349
  16.5 0.0 collective-permute-start.5
  16.5 3.1 %collective-permute-done.2.far_apart = bf16[48,4608]{1,0:T(8,128)(2,1)S(1)} collective-permute-done((bf16[48,4608]{1,0:T(8,128)(2,1)S(1)}, bf16[48,4608]{1,0:T(8,128)(2,1)S(1)}, u32[]{:S(2)}, u32[]{:S(2)}) %collective-permute-start.2) | collective-permute-done | bytes 442400 | tf_op jit(solution)/shard_map/ppermute | solution.py:349
  19.6 0.0 collective-permute-done.3.far_beside
  19.6 0.7 %shard_map.107.own = f32[64,4608]{1,0:T(8,128)S(1)} custom-call(bf16[384,128]{1,0:T(8,128)(2,1)S(1)} %get-tuple-element.18.matrix, bf16[64,160]{1,0:T(8,128)(2,1)S(1)} %get-tuple-element.19.weights, bf16[16,4608]{1,0:T(8,128)(2,1)S(1)} %get-tuple-element.21.first, bf16[16,4608]{1,0:T(8,128)(2,1)S(1)} %get-tuple-element.22.second, ...), custom_call_target="tpu_custom_call" | custom-call | tf_op jit(solution)/shard_map/pallas_call | solution.py:436
  20.3 0.0 collective-permute-done.4.first
  20.3 1.3 %collective-permute-done.5.second = bf16[16,4608]{1,0:T(8,128)(2,1)S(1)} collective-permute-done((bf16[16,4608]{1,0:T(8,128)(2,1)S(1)}, bf16[16,4608]{1,0:T(8,128)(2,1)S(1)}, u32[]{:S(2)}, u32[]{:S(2)}) %collective-permute-start.5) | collective-permute-done | bytes 147488 | tf_op jit(solution)/shard_map/ppermute | solution.py:349
  21.6 3.9 %shard_map.108 = (bf16[32,9216]{1,0:T(8,128)(2,1)}, bf16[32,9216]{1,0:T(8,128)(2,1)}) custom-call(bf16[64,64]{1,0:T(8,128)(2,1)S(1)} %get-tuple-element.16.weights, bf16[512,512]{1,0:T(8,128)(2,1)S(1)} %get-tuple-element.17.swapper, f32[64,4608]{1,0:T(8,128)S(1)} %shard_map.107.own, bf16[16,4608]{1,0:T(8,128)(2,1)S(1)} %collective-permute-done.4.first, ...), custom_call_target="tpu_custom_call" | custom-call | tf_op jit(solution)/shard_map/pallas_call | solution.py:447
Async XLA Ops:
  5.2 5.3 %collective-permute-start = (bf16[32,4608]{1,0:T(8,128)(2,1)S(1)}, bf16[32,4608]{1,0:T(8,128)(2,1)S(1)}, u32[]{:S(2)}, u32[]{:S(2)}) collective-permute-start(bf16[32,4608]{1,0:T(8,128)(2,1)S(1)} %get-tuple-element.15.near), channel_id=1, source_target_pairs={{0,4},{1,5},{2,6},{3,7},{4,0},{5,1},{6,2},{7,3},{8,12},{9,13},{10,... | collective-permute-start | bytes 884744 | tf_op jit(solution)/shard_map/ppermute | solution.py:349
  5.3 9.6 %collective-permute-start.1 = (bf16[32,4608]{1,0:T(8,128)(2,1)S(1)}, bf16[32,4608]{1,0:T(8,128)(2,1)S(1)}, u32[]{:S(2)}, u32[]{:S(2)}) collective-permute-start(bf16[32,4608]{1,0:T(8,128)(2,1)S(1)} %get-tuple-element.15.near), channel_id=1, source_target_pairs={{0,1},{1,0},{2,3},{3,2},{4,8},{5,9},{6,10},{7,11},{8,4},{9,5},{10,... | collective-permute-start | bytes 884744 | tf_op jit(solution)/shard_map/ppermute | solution.py:349
  7.7 11.9 %collective-permute-start.2 = (bf16[48,4608]{1,0:T(8,128)(2,1)S(1)}, bf16[48,4608]{1,0:T(8,128)(2,1)S(1)}, u32[]{:S(2)}, u32[]{:S(2)}) collective-permute-start(bf16[48,4608]{1,0:T(8,128)(2,1)S(1)} %get-tuple-element.23.far), channel_id=1, source_target_pairs={{0,1},{1,0},{2,3},{3,2},{4,8},{5,9},{6,10},{7,11},{8,4},{9,5},{10,... | collective-permute-start | bytes 1327112 | tf_op jit(solution)/shard_map/ppermute | solution.py:349
  10.5 9.1 %collective-permute-start.3 = (bf16[48,4608]{1,0:T(8,128)(2,1)S(1)}, bf16[48,4608]{1,0:T(8,128)(2,1)S(1)}, u32[]{:S(2)}, u32[]{:S(2)}) collective-permute-start(bf16[48,4608]{1,0:T(8,128)(2,1)S(1)} %get-tuple-element.23.far), channel_id=1, source_target_pairs={{0,4},{1,5},{2,6},{3,7},{4,0},{5,1},{6,2},{7,3},{8,12},{9,13},{10,... | collective-permute-start | bytes 1327112 | tf_op jit(solution)/shard_map/ppermute | solution.py:349
  15.1 5.2 %collective-permute-start.4 = (bf16[16,4608]{1,0:T(8,128)(2,1)S(1)}, bf16[16,4608]{1,0:T(8,128)(2,1)S(1)}, u32[]{:S(2)}, u32[]{:S(2)}) collective-permute-start(bf16[16,4608]{1,0:T(8,128)(2,1)S(1)} %get-tuple-element.21.first), channel_id=1, source_target_pairs={{0,1},{1,0},{2,3},{3,2},{4,5},{5,4},{6,7},{7,6},{8,9},{9,8},{10,11... | collective-permute-start | bytes 442376 | tf_op jit(solution)/shard_map/ppermute | solution.py:349
  16.5 5.1 %collective-permute-start.5 = (bf16[16,4608]{1,0:T(8,128)(2,1)S(1)}, bf16[16,4608]{1,0:T(8,128)(2,1)S(1)}, u32[]{:S(2)}, u32[]{:S(2)}) collective-permute-start(bf16[16,4608]{1,0:T(8,128)(2,1)S(1)} %get-tuple-element.22.second), channel_id=1, source_target_pairs={{0,4},{1,2},{2,1},{3,7},{4,0},{5,6},{6,5},{7,3},{8,12},{9,10},{10,... | collective-permute-start | bytes 442376 | tf_op jit(solution)/shard_map/ppermute | solution.py:349

commit v6 on v5

--- a/solution.py
+++ b/solution.py
@@ -19,6 +19,7 @@
 NEAR = 16
 SPAN = NEAR * PAIRS
 PITCH = PAIRS + 1
+TALL = 8 * ((NEAR + 1) * PITCH // 8 + 1)
 TILES = SPAN // LANES
 QUADS = PAIRS // GROUPS
 WIDTH = PAIRS * ROWS
@@ -383,7 +384,7 @@
 
 
 def on_device(green, sigma_in, neighbours, coupling, send_down, send_up, offsets, w_emit, w_absorb):
-    tall = shape_of(NEAR * PITCH, LANES, kind=F32)
+    tall = shape_of(TALL, LANES, kind=F32)
     half = shape_of(2 * EDGE, WIDTH)
     edge = shape_of(EDGE, WIDTH)
     green_t, sigma_t, near, far, once, swapper = pl.pallas_call(
@@ -450,9 +451,9 @@
         in_specs=vmem(7),
         out_specs=tuple(anywhere(2)),
         scratch_shapes=[
-            pltpu.VMEM((NEAR * PITCH, LANES), F32),
-            pltpu.VMEM((NEAR * PITCH, LANES), F32),
-            pltpu.VMEM((NEAR * PITCH, LANES), F32),
+            pltpu.VMEM((TALL, LANES), F32),
+            pltpu.VMEM((TALL, LANES), F32),
+            pltpu.VMEM((TALL, LANES), F32),
             pltpu.VMEM((ROWS, ATOMS * PAIRS), BF16),
             pltpu.VMEM((ROWS, ATOMS * PAIRS), BF16),
             pltpu.SemaphoreType.DMA((2 * GROUPS,)),

time: 25.7 us -> 25.7 us (level)
  no operation moved by 1% of the time
where the time goes in v6:
time: 25.7 us; the launch traced here: 25.6 us
  Pallas kernels  10.7 us (42%)
  waiting for transfers between devices  7.58 us (29%)
  starting transfers between devices  6.62 us (26%)
  between operations  0.67 us (3%)
    ppermute x6, waiting for transfers between devices, pair_up(): return lax.ppermute(block, ('energy', 'slab'), pairs)  7.58 us
    ppermute x6, starting transfers between devices, pair_up(): return lax.ppermute(block, ('energy', 'slab'), pairs)  6.62 us
    pallas_call x1, Pallas kernels, on_device(): pl.pallas_call(lesser_kernel, out_shape=(tall, tall, half, shape_of(REST,...  4.59 us
    pallas_call x1, Pallas kernels, on_device(): pl.pallas_call(final_kernel, out_shape=(flat, flat), in_specs=vmem(7), ou...  3.94 us
    pallas_call x1, Pallas kernels, on_device(): pl.pallas_call(here_kernel, out_shape=(shape_of(3 * LANES, LANES), shape_...  1.26 us
    pallas_call x1, Pallas kernels, on_device(): pl.pallas_call(far_kernel, out_shape=shape_of(ATOMS, WIDTH, kind=F32), in...  0.69 us
  transfers between devices with their start and end apart: 6, of which 3 were waited for; matrix products, arithmetic and copies ran while one was open for 0% of the time, Pallas kernels for 8%

profile of v6, /device:TPU:144, one launch (start us, length us, event | category | flops | bytes accessed | tf_op | source)
XLA Modules:
  0.0 25.6 jit_solution(9122803321003785788)
XLA Ops:
  0.6 4.6 %shard_map.104 = (f32[2472,128]{1,0:T(8,128)S(1)}, f32[2472,128]{1,0:T(8,128)S(1)}, bf16[32,4608]{1,0:T(8,128)(2,1)S(1)}, bf16[48,4608]{1,0:T(8,128)(2,1)S(1)}, ...) custom-call(bf16[32,9216]{1,0:T(8,128)(2,1)} %green.1, bf16[32,9216]{1,0:T(8,128)(2,1)} %sigma_in.1, ...), custom_call_target="tpu_custom_call" | custom-call | tf_op jit(solution)/shard_map/pallas_call | solution.py:390
  5.2 0.1 collective-permute-start
  5.3 2.4 %collective-permute-start.1 = (bf16[32,4608]{1,0:T(8,128)(2,1)S(1)}, bf16[32,4608]{1,0:T(8,128)(2,1)S(1)}, u32[]{:S(2)}, u32[]{:S(2)}) collective-permute-start(bf16[32,4608]{1,0:T(8,128)(2,1)S(1)} %get-tuple-element.15.near), channel_id=1, source_target_pairs={{0,1},{1,0},{2,3},{3,2},{4,8},{5,9},{6,10},{7,11},{8,4},{9,5},{10,... | collective-permute-start | bytes 884744 | tf_op jit(solution)/shard_map/ppermute | solution.py:350
  7.7 2.7 %collective-permute-start.2 = (bf16[48,4608]{1,0:T(8,128)(2,1)S(1)}, bf16[48,4608]{1,0:T(8,128)(2,1)S(1)}, u32[]{:S(2)}, u32[]{:S(2)}) collective-permute-start(bf16[48,4608]{1,0:T(8,128)(2,1)S(1)} %get-tuple-element.23.far), channel_id=1, source_target_pairs={{0,1},{1,0},{2,3},{3,2},{4,8},{5,9},{6,10},{7,11},{8,4},{9,5},{10,... | collective-permute-start | bytes 1327112 | tf_op jit(solution)/shard_map/ppermute | solution.py:350
  10.5 0.0 collective-permute-start.3
  10.5 0.0 collective-permute-done.near_beside
  10.5 1.3 %shard_map.105 = (bf16[384,128]{1,0:T(8,128)(2,1)S(1)}, bf16[64,160]{1,0:T(8,128)(2,1)S(1)}, bf16[64,64]{1,0:T(8,128)(2,1)S(1)}, f32[32,4608]{1,0:T(8,128)S(1)}) custom-call(s32[16]{0:T(128)} %offset_list.1, f32[16]{0:T(128)} %emit_list.1, f32[16]{0:T(128)} %absorb_list.1, s32[8,64]{1,0:T(8,128)} %bitcast.2, f32[8,64]{1,0:T(8,128)} %bitcast.3, ...), custom_call_target="tpu_custom_call" | custom-call | tf_op jit(solution)/shard_map/pallas_call | solution.py:412
  11.8 3.1 %collective-permute-done.1.near_apart = bf16[32,4608]{1,0:T(8,128)(2,1)S(1)} collective-permute-done((bf16[32,4608]{1,0:T(8,128)(2,1)S(1)}, bf16[32,4608]{1,0:T(8,128)(2,1)S(1)}, u32[]{:S(2)}, u32[]{:S(2)}) %collective-permute-start.1) | collective-permute-done | bytes 294944 | tf_op jit(solution)/shard_map/ppermute | solution.py:350
  14.9 0.2 shard_map.106
  15.1 1.4 %collective-permute-start.4 = (bf16[16,4608]{1,0:T(8,128)(2,1)S(1)}, bf16[16,4608]{1,0:T(8,128)(2,1)S(1)}, u32[]{:S(2)}, u32[]{:S(2)}) collective-permute-start(bf16[16,4608]{1,0:T(8,128)(2,1)S(1)} %get-tuple-element.21.first), channel_id=1, source_target_pairs={{0,1},{1,0},{2,3},{3,2},{4,5},{5,4},{6,7},{7,6},{8,9},{9,8},{10,11... | collective-permute-start | bytes 442376 | tf_op jit(solution)/shard_map/ppermute | solution.py:350
  16.5 0.0 collective-permute-start.5
  16.5 3.1 %collective-permute-done.2.far_apart = bf16[48,4608]{1,0:T(8,128)(2,1)S(1)} collective-permute-done((bf16[48,4608]{1,0:T(8,128)(2,1)S(1)}, bf16[48,4608]{1,0:T(8,128)(2,1)S(1)}, u32[]{:S(2)}, u32[]{:S(2)}) %collective-permute-start.2) | collective-permute-done | bytes 442400 | tf_op jit(solution)/shard_map/ppermute | solution.py:350
  19.6 0.0 collective-permute-done.3.far_beside
  19.6 0.7 %shard_map.107.own = f32[64,4608]{1,0:T(8,128)S(1)} custom-call(bf16[384,128]{1,0:T(8,128)(2,1)S(1)} %get-tuple-element.18.matrix, bf16[64,160]{1,0:T(8,128)(2,1)S(1)} %get-tuple-element.19.weights, bf16[16,4608]{1,0:T(8,128)(2,1)S(1)} %get-tuple-element.21.first, bf16[16,4608]{1,0:T(8,128)(2,1)S(1)} %get-tuple-element.22.second, ...), custom_call_target="tpu_custom_call" | custom-call | tf_op jit(solution)/shard_map/pallas_call | solution.py:437
  20.3 0.0 collective-permute-done.4.first
  20.3 1.3 %collective-permute-done.5.second = bf16[16,4608]{1,0:T(8,128)(2,1)S(1)} collective-permute-done((bf16[16,4608]{1,0:T(8,128)(2,1)S(1)}, bf16[16,4608]{1,0:T(8,128)(2,1)S(1)}, u32[]{:S(2)}, u32[]{:S(2)}) %collective-permute-start.5) | collective-permute-done | bytes 147488 | tf_op jit(solution)/shard_map/ppermute | solution.py:350
  21.6 3.9 %shard_map.108 = (bf16[32,9216]{1,0:T(8,128)(2,1)}, bf16[32,9216]{1,0:T(8,128)(2,1)}) custom-call(bf16[64,64]{1,0:T(8,128)(2,1)S(1)} %get-tuple-element.16.weights, bf16[512,512]{1,0:T(8,128)(2,1)S(1)} %get-tuple-element.17.swapper, f32[64,4608]{1,0:T(8,128)S(1)} %shard_map.107.own, bf16[16,4608]{1,0:T(8,128)(2,1)S(1)} %collective-permute-done.4.first, ...), custom_call_target="tpu_custom_call" | custom-call | tf_op jit(solution)/shard_map/pallas_call | solution.py:448
Async XLA Ops:
  5.2 5.3 %collective-permute-start = (bf16[32,4608]{1,0:T(8,128)(2,1)S(1)}, bf16[32,4608]{1,0:T(8,128)(2,1)S(1)}, u32[]{:S(2)}, u32[]{:S(2)}) collective-permute-start(bf16[32,4608]{1,0:T(8,128)(2,1)S(1)} %get-tuple-element.15.near), channel_id=1, source_target_pairs={{0,4},{1,5},{2,6},{3,7},{4,0},{5,1},{6,2},{7,3},{8,12},{9,13},{10,... | collective-permute-start | bytes 884744 | tf_op jit(solution)/shard_map/ppermute | solution.py:350
  5.3 9.6 %collective-permute-start.1 = (bf16[32,4608]{1,0:T(8,128)(2,1)S(1)}, bf16[32,4608]{1,0:T(8,128)(2,1)S(1)}, u32[]{:S(2)}, u32[]{:S(2)}) collective-permute-start(bf16[32,4608]{1,0:T(8,128)(2,1)S(1)} %get-tuple-element.15.near), channel_id=1, source_target_pairs={{0,1},{1,0},{2,3},{3,2},{4,8},{5,9},{6,10},{7,11},{8,4},{9,5},{10,... | collective-permute-start | bytes 884744 | tf_op jit(solution)/shard_map/ppermute | solution.py:350
  7.7 11.9 %collective-permute-start.2 = (bf16[48,4608]{1,0:T(8,128)(2,1)S(1)}, bf16[48,4608]{1,0:T(8,128)(2,1)S(1)}, u32[]{:S(2)}, u32[]{:S(2)}) collective-permute-start(bf16[48,4608]{1,0:T(8,128)(2,1)S(1)} %get-tuple-element.23.far), channel_id=1, source_target_pairs={{0,1},{1,0},{2,3},{3,2},{4,8},{5,9},{6,10},{7,11},{8,4},{9,5},{10,... | collective-permute-start | bytes 1327112 | tf_op jit(solution)/shard_map/ppermute | solution.py:350
  10.5 9.1 %collective-permute-start.3 = (bf16[48,4608]{1,0:T(8,128)(2,1)S(1)}, bf16[48,4608]{1,0:T(8,128)(2,1)S(1)}, u32[]{:S(2)}, u32[]{:S(2)}) collective-permute-start(bf16[48,4608]{1,0:T(8,128)(2,1)S(1)} %get-tuple-element.23.far), channel_id=1, source_target_pairs={{0,4},{1,5},{2,6},{3,7},{4,0},{5,1},{6,2},{7,3},{8,12},{9,13},{10,... | collective-permute-start | bytes 1327112 | tf_op jit(solution)/shard_map/ppermute | solution.py:350
  15.1 5.2 %collective-permute-start.4 = (bf16[16,4608]{1,0:T(8,128)(2,1)S(1)}, bf16[16,4608]{1,0:T(8,128)(2,1)S(1)}, u32[]{:S(2)}, u32[]{:S(2)}) collective-permute-start(bf16[16,4608]{1,0:T(8,128)(2,1)S(1)} %get-tuple-element.21.first), channel_id=1, source_target_pairs={{0,1},{1,0},{2,3},{3,2},{4,5},{5,4},{6,7},{7,6},{8,9},{9,8},{10,11... | collective-permute-start | bytes 442376 | tf_op jit(solution)/shard_map/ppermute | solution.py:350
  16.5 5.1 %collective-permute-start.5 = (bf16[16,4608]{1,0:T(8,128)(2,1)S(1)}, bf16[16,4608]{1,0:T(8,128)(2,1)S(1)}, u32[]{:S(2)}, u32[]{:S(2)}) collective-permute-start(bf16[16,4608]{1,0:T(8,128)(2,1)S(1)} %get-tuple-element.22.second), channel_id=1, source_target_pairs={{0,4},{1,2},{2,1},{3,7},{4,0},{5,6},{6,5},{7,3},{8,12},{9,10},{10,... | collective-permute-start | bytes 442376 | tf_op jit(solution)/shard_map/ppermute | solution.py:350
